TPU v7x, 256 devices: a whole 4x4x8 slice. The times are simulated.
256 devices in a mesh: chol: 8 (over z), vol: 32 (over y, x, core).
Axes of the slice: x: 4, y: 4, z: 8, core: 2. Of those that a mesh axis runs over, the one named last changes fastest.
Arguments:
- diag_block: float32 [1024, 1024], P('vol'), as said below
- rhs_diag: float32 [3, 1024], P(None, 'vol'), may hold values from -0.3125 to 0.3125
- panel_block: float32 [32768, 1024], P(('chol', 'vol')), may hold values from -0.625 to 0.625
- rhs_panel: float32 [3, 32768], P(None, ('chol', 'vol')), may hold values from -1.25 to 1.25
- trail: float32 [32768, 1024], P(('chol', 'vol')), may hold values from -6 to 6
- ctrl_xyz: float32 [3, 32768], P(None, ('chol', 'vol')), may hold values from 0 to 256, as said below
- node_xyz: float32 [3, 2097152], P(None, ('chol', 'vol')), may hold values from 0 to 256, as said below
- tile_blocks: int32 [16384, 8], P(('chol', 'vol')), may hold values from 0 to 255, as said below
- tile_count: int32 [16384], P(('chol', 'vol')), may hold values from 3 to 8, as said below
- face_area: float32 [3, 6, 2097152], P(None, None, ('chol', 'vol')), may hold values from -1.25 to 1.25
- edge_nbr: int32 [6, 2097152], P(None, ('chol', 'vol')), may hold values from 0 to 8447, as said below
- old_volume: float32 [2097152], P(('chol', 'vol')), may hold values from 0.5 to 2
Outputs:
- trail_out: float32 [32768, 1024], P(('chol', 'vol'))
- node_disp: float32 [3, 2097152], P(None, ('chol', 'vol'))
- new_volume: float32 [2097152], P(('chol', 'vol'))
Inputs may be any that keep to these rules, and one draw needn't show every extreme that they name: diag_block is symmetric and each diagonal entry exceeds the sum of magnitudes of the other entries of its row by 0.05 or more. tile_count gives how many leading slots of a tile's list are used. `tile_blocks`: the used slots of a tile name consecutive control blocks in increasing order; the unused ones repeat its first block. `ctrl_xyz`: the first coordinate of control point j lies in [j // 128, j // 128 + 1). `node_xyz`: the first coordinate is a position along the hull in units of one control block's length. For node n at position p of its partition, edge_nbr[e, n] - p - 128 is a nonzero offset of at most 128 in magnitude.
All inputs are finite; a program needn't handle non-finite values.
Results may differ from a plain program's by a relative error of at most 0.0003.
Values sent between devices are 32-bit elements; how exact they have to be, the bound alone decides.
No kernel may reach another device: no remote copies, remote signals or barrier semaphores. Data moves between devices by JAX's collectives and lax.ppermute only.
A program may use at most 128 MiB of HBM per device.

v0:
```python
import jax
import jax.numpy as jnp
from jax import lax
from jax.sharding import PartitionSpec as P

HALO = 128


highest_mode = lax.Precision.HIGHEST
support_radius = 1.25


def with_halo(block, sides, width):
    for axis, dim in sides:
        count = lax.axis_size(axis)
        forward = [(i, i + 1) for i in range(count - 1)]
        backward = [(target, source) for source, target in forward]
        low = lax.ppermute(
            lax.slice_in_dim(block, block.shape[dim] - width, None, axis=dim), axis, forward
        )
        high = lax.ppermute(lax.slice_in_dim(block, 0, width, axis=dim), axis, backward)
        block = jnp.concatenate([low, block, high], axis=dim)
    return block


def wendland(dist_sq):
    scaled = jnp.sqrt(dist_sq) / support_radius
    remain = jnp.maximum(1.0 - scaled, 0.0)
    return remain**4 * (4.0 * scaled + 1.0)


def slot_term(tile_xyz, chosen, live_mask, blocks_xyz, blocks_weight):
    near_xyz = blocks_xyz[:, chosen]
    near_weight = blocks_weight[:, chosen]
    dist_sq = jnp.zeros((tile_xyz.shape[1], 128, 128), jnp.float32)
    for axis_pos in range(3):
        differ = tile_xyz[axis_pos][:, :, None] - near_xyz[axis_pos][:, None, :]
        dist_sq = dist_sq + differ * differ
    kernel = wendland(dist_sq)
    term = jnp.einsum("tnc,atc->atn", kernel, near_weight, precision=highest_mode)
    return term * live_mask[None, :, None]


def per_device(
    diag_block,
    rhs_diag,
    panel_block,
    rhs_panel,
    trail,
    ctrl_xyz,
    node_xyz,
    tile_blocks,
    tile_count,
    face_area,
    edge_nbr,
    old_volume,
):
    whole_diag, whole_rhs = (
        lax.all_gather(diag_block, "vol", axis=0, tiled=True),
        lax.all_gather(rhs_diag, "vol", axis=1, tiled=True),
    )
    factor = jnp.linalg.cholesky(whole_diag)
    lower_panel = jax.scipy.linalg.solve_triangular(factor, panel_block.T, lower=True).T
    forward = jax.scipy.linalg.solve_triangular(factor, whole_rhs.T, lower=True)
    ctrl_weight = rhs_panel - jnp.dot(lower_panel, forward, precision=highest_mode).T
    gathered_xyz, gathered_weight = (
        lax.all_gather(ctrl_xyz, ("chol", "vol"), axis=1, tiled=True),
        lax.all_gather(ctrl_weight, ("chol", "vol"), axis=1, tiled=True),
    )
    products = jnp.dot(
        lower_panel,
        lax.all_gather(lower_panel, "chol", axis=0, tiled=True).T,
        precision=highest_mode,
    )
    trail_out = trail - products
    blocks_xyz = gathered_xyz.reshape(3, -1, 128)
    blocks_weight = gathered_weight.reshape(3, -1, 128)
    tile_xyz = node_xyz.reshape(3, -1, 128)
    tile_total = tile_xyz.shape[1]
    zeros_start = jnp.zeros((3, tile_total, 128), jnp.float32)
    running = zeros_start
    for slot_index in range(tile_blocks.shape[1]):
        live_mask = (slot_index < tile_count).astype(jnp.float32)
        running = running + slot_term(
            tile_xyz, tile_blocks[:, slot_index], live_mask, blocks_xyz, blocks_weight
        )
    node_disp = running.reshape(3, -1)
    extended = with_halo(node_disp, (("vol", 1),), HALO)
    across_disp = extended[:, edge_nbr]
    flux = jnp.sum(face_area * (node_disp[:, None, :] + across_disp), axis=(0, 1))
    new_volume = old_volume + 0.5 * flux
    return (trail_out, node_disp, new_volume)


def solution(mesh):
    return jax.shard_map(
        per_device,
        mesh=mesh,
        in_specs=(
            P("vol", None),
            P(None, "vol"),
            P(("chol", "vol"), None),
            P(None, ("chol", "vol")),
            P(("chol", "vol"), None),
            P(None, ("chol", "vol")),
            P(None, ("chol", "vol")),
            P(("chol", "vol"), None),
            P(("chol", "vol")),
            P(None, None, ("chol", "vol")),
            P(None, ("chol", "vol")),
            P(("chol", "vol")),
        ),
        out_specs=(P(("chol", "vol"), None), P(None, ("chol", "vol")), P(("chol", "vol"))),
        check_vma=False,
    )
```

profile of v0, /device:TPU:1, one launch (start us, length us, event | category | flops | bytes accessed | tf_op | source)
XLA Modules:
  0.0 814.4 jit_solution(8358613724519774428)
XLA Ops:
  8.0 25.8 %all-gather = f32[32,32,3]{1,2,0:T(4,128)S(1)} all-gather(f32[1,32,3]{1,2,0:T(4,128)} %bitcast.337), channel_id=1, replica_groups=mesh['chol'=8,'vol'=32] {'vol'}, dimensions={0}, use_global_device_ids=true | all-gather | bytes 12672 | tf_op jit(solution)/shard_map/all_gather | solution.py:60
  35.6 1.2 copy.43
  37.9 70.6 %all_gather.19 = f32[3,32768]{1,0:T(4,128)S(1)} all-gather(f32[3,128]{1,0:T(4,128)} %param.17), channel_id=1, replica_groups=mesh['chol'=8,'vol'=32] {'chol','vol'}, dimensions={1}, use_global_device_ids=true | all-gather | bytes 394752 | tf_op jit(solution)/shard_map/all_gather | solution.py:67
  114.6 5.5 copy.42
  120.1 4.4 fusion
  124.6 1.9 copy-done.1
  126.5 11.7 %cholesky.223 = f32[128,128]{1,0:T(8,128)S(1)} custom-call(f32[128,128]{1,0:T(8,128)S(1)} %cholesky.580), custom_call_target="Cholesky" | custom-call | tf_op jit(solution)/shard_map/jit(cholesky)/cholesky | solution.py:62
  138.3 9.8 %custom-call.66 = f32[1,128,128]{1,2,0:T(8,128)S(1)} custom-call(f32[1,128,128]{2,1,0:T(8,128)S(1)} %get-tuple-element.107), custom_call_target="InvertDiagBlocksLowerTriangular" | custom-call | tf_op jit(solution)/shard_map/jit(cholesky)/cholesky | solution.py:62
  148.1 2.5 cholesky.255
  150.6 2.4 constant_dynamic-update-slice_fusion.57
  153.0 1.5 convolution_subtract_fusion.1
  154.5 11.9 %cholesky.244 = f32[128,128]{1,0:T(8,128)S(1)} custom-call(f32[128,128]{1,0:T(8,128)S(1)} %cholesky.584), custom_call_target="Cholesky" | custom-call | tf_op jit(solution)/shard_map/jit(cholesky)/cholesky | solution.py:62
  167.1 9.8 %custom-call.67 = f32[1,128,128]{1,2,0:T(8,128)S(1)} custom-call(f32[1,128,128]{2,1,0:T(8,128)S(1)} %get-tuple-element.104), custom_call_target="InvertDiagBlocksLowerTriangular" | custom-call | tf_op jit(solution)/shard_map/jit(cholesky)/cholesky | solution.py:62
  176.9 1.3 convolution_dynamic-update-slice_fusion
  178.2 2.1 convolution_subtract_fusion.2
  180.3 11.7 %cholesky.468 = f32[128,128]{1,0:T(8,128)S(1)} custom-call(f32[128,128]{1,0:T(8,128)S(1)} %cholesky.589), custom_call_target="Cholesky" | custom-call | tf_op jit(solution)/shard_map/jit(cholesky)/cholesky | solution.py:62
  193.3 9.8 %custom-call.68 = f32[1,128,128]{1,2,0:T(8,128)S(1)} custom-call(f32[1,128,128]{2,1,0:T(8,128)S(1)} %get-tuple-element.101), custom_call_target="InvertDiagBlocksLowerTriangular" | custom-call | tf_op jit(solution)/shard_map/jit(cholesky)/cholesky | solution.py:62
  203.1 1.2 convolution_dynamic-update-slice_fusion.1
  204.2 2.3 convolution_subtract_fusion.3
  206.6 12.1 %cholesky.487 = f32[128,128]{1,0:T(8,128)S(1)} custom-call(f32[128,128]{1,0:T(8,128)S(1)} %cholesky.594), custom_call_target="Cholesky" | custom-call | tf_op jit(solution)/shard_map/jit(cholesky)/cholesky | solution.py:62
  220.0 9.8 %custom-call.69 = f32[1,128,128]{1,2,0:T(8,128)S(1)} custom-call(f32[1,128,128]{2,1,0:T(8,128)S(1)} %get-tuple-element.98), custom_call_target="InvertDiagBlocksLowerTriangular" | custom-call | tf_op jit(solution)/shard_map/jit(cholesky)/cholesky | solution.py:62
  231.0 2.3 convolution_subtract_fusion.4
  233.3 11.7 %cholesky.506 = f32[128,128]{1,0:T(8,128)S(1)} custom-call(f32[128,128]{1,0:T(8,128)S(1)} %cholesky.599), custom_call_target="Cholesky" | custom-call | tf_op jit(solution)/shard_map/jit(cholesky)/cholesky | solution.py:62
  246.4 9.9 %custom-call.70 = f32[1,128,128]{1,2,0:T(8,128)S(1)} custom-call(f32[1,128,128]{2,1,0:T(8,128)S(1)} %get-tuple-element.95), custom_call_target="InvertDiagBlocksLowerTriangular" | custom-call | tf_op jit(solution)/shard_map/jit(cholesky)/cholesky | solution.py:62
  257.3 2.3 convolution_subtract_fusion.5
  259.6 11.7 %cholesky.526 = f32[128,128]{1,0:T(8,128)S(1)} custom-call(f32[128,128]{1,0:T(8,128)S(1)} %cholesky.604), custom_call_target="Cholesky" | custom-call | tf_op jit(solution)/shard_map/jit(cholesky)/cholesky | solution.py:62
  272.6 9.8 %custom-call.71 = f32[1,128,128]{1,2,0:T(8,128)S(1)} custom-call(f32[1,128,128]{2,1,0:T(8,128)S(1)} %get-tuple-element.92), custom_call_target="InvertDiagBlocksLowerTriangular" | custom-call | tf_op jit(solution)/shard_map/jit(cholesky)/cholesky | solution.py:62
  283.3 2.0 convolution_subtract_fusion.6
  285.4 11.9 %cholesky.546 = f32[128,128]{1,0:T(8,128)S(1)} custom-call(f32[128,128]{1,0:T(8,128)S(1)} %cholesky.609), custom_call_target="Cholesky" | custom-call | tf_op jit(solution)/shard_map/jit(cholesky)/cholesky | solution.py:62
  298.6 9.8 %custom-call.72 = f32[1,128,128]{1,2,0:T(8,128)S(1)} custom-call(f32[1,128,128]{2,1,0:T(8,128)S(1)} %get-tuple-element.89), custom_call_target="InvertDiagBlocksLowerTriangular" | custom-call | tf_op jit(solution)/shard_map/jit(cholesky)/cholesky | solution.py:62
  309.3 1.9 convolution_subtract_fusion.12
  311.1 11.7 %cholesky.564 = f32[128,128]{1,0:T(8,128)S(1)} custom-call(f32[128,128]{1,0:T(8,128)S(1)} %convolution_subtract_fusion.12), custom_call_target="Cholesky" | custom-call | tf_op jit(solution)/shard_map/jit(cholesky)/cholesky | solution.py:62
  329.8 4.8 select_select_fusion
  334.6 27.6 %while.1 = (s32[]{:T(128)}, f32[1024,1024]{1,0:T(8,128)}, s32[8,2]{0,1:T(2,128)S(1)}, f32[8,128,128]{2,1,0:T(8,128)}, s32[]{:T(128)}) while((s32[]{:T(128)}, f32[1024,1024]{1,0:T(8,128)}, s32[8,2]{0,1:T(2,128)S(1)}, f32[8,128,128]{2,1,0:T(8,128)}, s32[]{:T(128)}) %tuple.128), condition=%wide.while_cond, body=%wide.while_body.sunk | while | flops 2 | bytes 132205 | solution.py:63
  335.2 2.9 bitcast_dynamic-update-slice_fusion.2
  338.7 2.9 bitcast_dynamic-update-slice_fusion.2
  342.1 2.9 bitcast_dynamic-update-slice_fusion.2
  345.6 2.9 bitcast_dynamic-update-slice_fusion.2
  349.1 2.9 bitcast_dynamic-update-slice_fusion.2
  352.5 2.9 bitcast_dynamic-update-slice_fusion.2
  356.0 2.9 bitcast_dynamic-update-slice_fusion.2
  359.4 2.8 bitcast_dynamic-update-slice_fusion.2
  362.2 79.8 %custom-call.73 = f32[8,128,128]{1,2,0:T(8,128)S(1)} custom-call(f32[8,128,128]{2,1,0:T(8,128)} %get-tuple-element.10), custom_call_target="InvertDiagBlocksLowerTriangular" | custom-call | tf_op jit(solution)/shard_map/jit(_solve_triangular)/triangular_solve | solution.py:63
  442.5 1.3 convolution_subtract_fusion.11
  444.1 1.2 convolution_subtract_fusion.10
  445.6 1.2 convolution_subtract_fusion.14
  447.1 1.3 convolution_subtract_fusion.13
  448.7 1.4 convolution_subtract_fusion.9
  456.3 65.6 %all_gather.18 = f32[3,32768]{1,0:T(4,128)S(1)} all-gather(f32[3,128]{1,0:T(4,128)S(1)} %convolution_subtract_fusion.21), channel_id=1, replica_groups=mesh['chol'=8,'vol'=32] {'chol','vol'}, dimensions={1}, use_global_device_ids=true | all-gather | bytes 394752 | tf_op jit(solution)/shard_map/all_gather | solution.py:68
  527.2 10.7 %fusion.231 = f32[64,3,128]{2,1,0:T(4,128)S(1)} fusion(f32[64,128]{1,0:T(8,128)S(1)} %bitcast.336, f32[64,128]{1,0:T(8,128)S(1)} %bitcast.335, f32[64,128]{1,0:T(8,128)S(1)} %bitcast.334, f32[64,128]{1,0:T(8,128)S(1)} %bitcast.306, f32[64,128]{1,0:T(8,128)S(1)} %bitcast.314, f32[64,128]{1,0:T(8,128)S(1)} %bitcast.298, f32[64,3,128]{2,1,0:T(4,128)S(1)} %gather_fusion.2, ...), kind=kOutput, calls=%fused_computation.261 | convolution fusion | flops 54550528 | bytes 393472 | tf_op jit(solution)/shard_map/tnc,atc->atn/dot_general | solution.py:40
  537.9 10.5 %fusion.228 = f32[64,3,128]{2,1,0:T(4,128)S(1)} fusion(f32[64,3,128]{2,1,0:T(4,128)S(1)} %fusion.231, f32[64,128]{1,0:T(8,128)S(1)} %bitcast.333, f32[64,128]{1,0:T(8,128)S(1)} %bitcast.307, f32[64,128]{1,0:T(8,128)S(1)} %bitcast.332, f32[64,128]{1,0:T(8,128)S(1)} %bitcast.315, f32[64,128]{1,0:T(8,128)S(1)} %bitcast.331, f32[64,128]{1,0:T(8,128)S(1)} %bitcast.299, ...), kind=kOutput, calls=%fused_computation.260 | convolution fusion | flops 54575104 | bytes 491776 | tf_op jit(solution)/shard_map/tnc,atc->atn/dot_general | solution.py:40
  548.4 10.5 %fusion.237 = f32[64,3,128]{2,1,0:T(4,128)S(1)} fusion(f32[64,3,128]{2,1,0:T(4,128)S(1)} %fusion.228, f32[64,128]{1,0:T(8,128)S(1)} %bitcast.330, f32[64,128]{1,0:T(8,128)S(1)} %bitcast.329, f32[64,128]{1,0:T(8,128)S(1)} %bitcast.328, f32[64,128]{1,0:T(8,128)S(1)} %bitcast.308, f32[64,128]{1,0:T(8,128)S(1)} %bitcast.316, f32[64,128]{1,0:T(8,128)S(1)} %bitcast.300, ...), kind=kOutput, calls=%fused_computation.263 | convolution fusion | flops 54575104 | bytes 491776 | tf_op jit(solution)/shard_map/tnc,atc->atn/dot_general | solution.py:40
  558.9 10.5 %fusion.243 = f32[64,3,128]{2,1,0:T(4,128)S(1)} fusion(f32[64,3,128]{2,1,0:T(4,128)S(1)} %fusion.237, f32[64,128]{1,0:T(8,128)S(1)} %bitcast.327, f32[64,128]{1,0:T(8,128)S(1)} %bitcast.326, f32[64,128]{1,0:T(8,128)S(1)} %bitcast.325, f32[64,128]{1,0:T(8,128)S(1)} %bitcast.309, f32[64,128]{1,0:T(8,128)S(1)} %bitcast.317, f32[64,128]{1,0:T(8,128)S(1)} %bitcast.301, ...), kind=kOutput, calls=%fused_computation.265 | convolution fusion | flops 54575104 | bytes 491776 | tf_op jit(solution)/shard_map/tnc,atc->atn/dot_general | solution.py:40
  569.5 10.5 %fusion.249 = f32[64,3,128]{2,1,0:T(4,128)S(1)} fusion(f32[64,3,128]{2,1,0:T(4,128)S(1)} %fusion.243, f32[64,128]{1,0:T(8,128)S(1)} %bitcast.324, f32[64,128]{1,0:T(8,128)S(1)} %bitcast.323, f32[64,128]{1,0:T(8,128)S(1)} %bitcast.322, f32[64,128]{1,0:T(8,128)S(1)} %bitcast.310, f32[64,128]{1,0:T(8,128)S(1)} %bitcast.318, f32[64,128]{1,0:T(8,128)S(1)} %bitcast.302, ...), kind=kOutput, calls=%fused_computation.267 | convolution fusion | flops 54575104 | bytes 491776 | tf_op jit(solution)/shard_map/tnc,atc->atn/dot_general | solution.py:40
  580.0 10.5 %fusion.255 = f32[64,3,128]{2,1,0:T(4,128)S(1)} fusion(f32[64,3,128]{2,1,0:T(4,128)S(1)} %fusion.249, f32[64,128]{1,0:T(8,128)S(1)} %bitcast.297, f32[64,128]{1,0:T(8,128)S(1)} %bitcast.296, f32[64,128]{1,0:T(8,128)S(1)} %bitcast.295, f32[64,128]{1,0:T(8,128)S(1)} %bitcast.311, f32[64,128]{1,0:T(8,128)S(1)} %bitcast.319, f32[64,128]{1,0:T(8,128)S(1)} %bitcast.303, ...), kind=kOutput, calls=%fused_computation.269 | convolution fusion | flops 54575104 | bytes 491776 | tf_op jit(solution)/shard_map/tnc,atc->atn/dot_general | solution.py:40
  590.5 10.5 %fusion.261 = f32[64,3,128]{2,1,0:T(4,128)S(1)} fusion(f32[64,3,128]{2,1,0:T(4,128)S(1)} %fusion.255, f32[64,128]{1,0:T(8,128)S(1)} %bitcast.294, f32[64,128]{1,0:T(8,128)S(1)} %bitcast.293, f32[64,128]{1,0:T(8,128)S(1)} %bitcast.292, f32[64,128]{1,0:T(8,128)S(1)} %bitcast.312, f32[64,128]{1,0:T(8,128)S(1)} %bitcast.320, f32[64,128]{1,0:T(8,128)S(1)} %bitcast.304, ...), kind=kOutput, calls=%fused_computation.271 | convolution fusion | flops 54575104 | bytes 491776 | tf_op jit(solution)/shard_map/tnc,atc->atn/dot_general | solution.py:40
  601.0 10.5 %fusion.270 = f32[3,8192]{1,0:T(4,128)S(1)} fusion(f32[64,3,128]{2,1,0:T(4,128)S(1)} %fusion.261, f32[64,128]{1,0:T(8,128)S(1)} %bitcast.291, f32[64,128]{1,0:T(8,128)S(1)} %bitcast.290, f32[64,128]{1,0:T(8,128)S(1)} %bitcast.289, f32[64,128]{1,0:T(8,128)S(1)} %bitcast.313, f32[64,128]{1,0:T(8,128)S(1)} %bitcast.321, f32[64,128]{1,0:T(8,128)S(1)} %bitcast.305, ...), kind=kOutput, calls=%fused_computation.274 | convolution fusion | flops 54575104 | bytes 491776 | tf_op jit(solution)/shard_map/tnc,atc->atn/dot_general | solution.py:40
  611.5 1.9 collective-permute-start
  613.5 2.4 collective-permute-start.1
  615.9 2.4 collective-permute-done.1
  618.4 2.7 copy.60
  621.1 164.1 %gather_fusion.16 = f32[49152,3]{1,0:T(8,128)} fusion(f32[3,8448]{0,1:T(8,128)} %copy.60, s32[49152]{0:T(1024)S(1)} %broadcast_clamp_fusion), kind=kCustom, calls=%fused_computation.16 | custom fusion | bytes 1376256 | tf_op jit(solution)/shard_map/gather | solution.py:89
  785.3 15.9 %copy.61 = f32[6,8192,3]{1,0,2:T(8,128)S(1)} copy(f32[6,8192,3]{2,1,0:T(8,128)} %bitcast.255) | data formatting | bytes 1179648 | tf_op jit(solution)/shard_map/gather | solution.py:89
  802.0 5.4 convolution_subtract_fusion
  (154 shorter events, 41.3 us)
Async XLA Ops:
  7.2 106.7 %copy-start.10 = (s32[64]{0:T(128)S(1)}, s32[64]{0:T(128)}, u32[]{:S(2)}) copy-start(s32[64]{0:T(128)} %param.20) | copy-start | bytes 772
  7.2 107.3 %copy-start.7 = (f32[3,8192]{1,0:T(4,128)S(1)}, f32[3,8192]{1,0:T(4,128)}, u32[]{:S(2)}) copy-start(f32[3,8192]{1,0:T(4,128)} %param.18) | copy-start | bytes 294916
  7.2 107.4 %all-gather.4.cloned.1.call-start = ((), (), s32[]{:S(2)}) async-start(), calls=%async_computation | async-start | bytes 4325376 | tf_op jit(solution)/shard_map/all_gather | solution.py:59
  7.9 794.1 %all-gather.6.cloned.1.call-start = ((), (), s32[]{:S(2)}) async-start(), calls=%async_computation.1 | async-start | bytes 4718592 | tf_op jit(solution)/shard_map/all_gather | solution.py:72
  124.6 2.0 copy-start.1
  442.0 8.5 %copy-start = (f32[1024,1024]{1,0:T(8,128)S(1)}, f32[1024,1024]{1,0:T(8,128)}, u32[]{:S(2)}) copy-start(f32[1024,1024]{1,0:T(8,128)} %get-tuple-element.216) | copy-start | bytes 12582916
  445.3 10.6 %copy-start.9 = (f32[3,128]{1,0:T(4,128)S(1)}, f32[3,128]{1,0:T(4,128)}, u32[]{:S(2)}) copy-start(f32[3,128]{1,0:T(4,128)} %param.15) | copy-start | bytes 4612
  455.9 71.3 %copy-start.2 = (f32[1024,128]{1,0:T(8,128)}, f32[1024,128]{1,0:T(8,128)S(1)}, u32[]{:S(2)}) copy-start(f32[1024,128]{1,0:T(8,128)S(1)} %convolution_dynamic-update-slice_fusion.5) | copy-start | bytes 1572868
  611.5 189.6 %copy-start.5 = (f32[3,8192]{1,0:T(4,128)}, f32[3,8192]{1,0:T(4,128)S(1)}, u32[]{:S(2)}) copy-start(f32[3,8192]{1,0:T(4,128)S(1)} %fusion.270) | copy-start | bytes 294916
  611.5 4.4 collective-permute-start
  613.5 4.9 collective-permute-start.1
  785.3 15.9 %copy-start.4 = (f32[3,6,8192]{2,1,0:T(8,128)S(1)}, f32[3,6,8192]{2,1,0:T(8,128)}, u32[]{:S(2)}) copy-start(f32[3,6,8192]{2,1,0:T(8,128)} %param.21) | copy-start | bytes 1769476
  785.3 16.1 %copy-start.8 = (f32[8192]{0:T(1024)S(1)}, f32[8192]{0:T(1024)}, u32[]{:S(2)}) copy-start(f32[8192]{0:T(1024)} %param.23) | copy-start | bytes 98308
  785.3 16.7 %copy-start.3 = (f32[1024,128]{1,0:T(8,128)S(1)}, f32[1024,128]{1,0:T(8,128)}, u32[]{:S(2)}) copy-start(f32[1024,128]{1,0:T(8,128)} %copy-done.2) | copy-start | bytes 1572868
  785.3 16.7 %copy-start.6 = (f32[128,1024]{1,0:T(8,128)S(1)}, f32[128,1024]{1,0:T(8,128)}, u32[]{:S(2)}) copy-start(f32[128,1024]{1,0:T(8,128)} %param.16) | copy-start | bytes 1572868
Sparse Core Ops, SparseCore 0:
  10.6 55.2 all-gather.3
  527.3 55.1 all-gather.5
where the time goes:
time: 821 us; the launch traced here: 814 us
  other arithmetic  264 us (32%)
  local copies, waits for them, and re-layouts  234 us (29%)
  blocking collectives  162 us (20%)
  matrix products  127 us (15%)
  between operations  19.9 us (2%)
    gather x2, local copies, waits for them, and re-layouts, per_device(): across_disp = extended[:, edge_nbr]  180 us
    another operation x30, other arithmetic, per_device(): factor = jnp.linalg.cholesky(whole_diag)  172 us
    another operation x3, other arithmetic, per_device(): jax.scipy.linalg.solve_triangular(factor, panel_block.T, lower=True)  84.6 us
    dot_general x8, matrix products, slot_term(): jnp.einsum('tnc,atc->atn', kernel, near_weight, precision=highest_mode)  84.3 us
    all_gather x1, blocking collectives, per_device(): lax.all_gather(ctrl_xyz, ('chol', 'vol'), axis=1, tiled=True)  70.6 us
    all_gather x1, blocking collectives, per_device(): lax.all_gather(ctrl_weight, ('chol', 'vol'), axis=1, tiled=True)  65.6 us
    another operation x24, local copies, waits for them, and re-layouts  27.5 us
    all_gather x1, blocking collectives, per_device(): lax.all_gather(rhs_diag, 'vol', axis=1, tiled=True)  25.8 us
  transfers between devices with their start and end apart: 4, of which 1 were waited for; matrix products, arithmetic and copies ran while one was open for 34% of the time, Pallas kernels for 0%

commit v1 on v0

v1 whole, which is shorter than its diff:
```python
import jax
import jax.numpy as jnp
from jax import lax
from jax.experimental import pallas as pl
from jax.experimental.pallas import tpu as pltpu
from jax.sharding import PartitionSpec as P

F32 = jnp.float32
BF16 = jnp.bfloat16
NN = (((1,), (0,)), ((), ()))
NT = (((1,), (1,)), ((), ()))
WIDE = 256
STEPS = 4
ORDER = 1024
SIDE = 256
VMEM = pl.BlockSpec(memory_space=pltpu.VMEM)


def split(value):
    high = value.astype(BF16)
    return high, (value - high.astype(F32)).astype(BF16)


def raw_dot(left, right, dims=NN):
    return lax.dot_general(left, right, dims, preferred_element_type=F32)


def product(left, right, dims=NN):
    left_high, left_low = left
    right_high, right_low = right
    return (
        raw_dot(left_high, right_low, dims) + raw_dot(left_low, right_high, dims)
    ) + raw_dot(left_high, right_high, dims)


def inverse(block):
    size = block.shape[0]
    row_id = lax.broadcasted_iota(jnp.int32, (size, size), 0)
    col_id = lax.broadcasted_iota(jnp.int32, (size, size), 1)
    on_diag = row_id == col_id
    only_diag = jnp.where(on_diag, block, 0.0)
    diag_col = jnp.sum(only_diag, axis=1, keepdims=True)
    diag_row = jnp.sum(only_diag, axis=0, keepdims=True)
    power = jnp.where(on_diag, 0.0, -block / diag_col)
    total = jnp.where(on_diag, 1.0, power)
    parts = split(power)
    power = product(parts, parts)

    def stage(power, total):
        parts = split(power)
        return product(parts, parts), total + product(split(total), parts)

    for _ in range(4):
        power, total = stage(power, total)
    total = total + product(split(total), split(power))

    def left_over(power):
        return size * jnp.max(jnp.abs(power)) ** 2

    def unfinished(state):
        return (state[2] > 1e-7) & (state[3] < 40)

    def more(state):
        power, total, _, count = state
        parts = split(power)
        power = product(parts, parts)
        total = total + product(split(total), split(power))
        return power, total, left_over(power), count + 1

    total = lax.while_loop(unfinished, more, (power, total, left_over(power), 0))[1]
    return total / diag_row


def factor_body(rows_ref, panel_ref, out_ref, m_ref, vh_ref, vl_ref):
    full = ORDER + SIDE
    half_row = lax.broadcasted_iota(jnp.int32, (128, 128), 0) // 64
    half_col = lax.broadcasted_iota(jnp.int32, (128, 128), 1) // 64
    lane = lax.broadcasted_iota(jnp.int32, (128, 128), 1)
    def rows_of(g, m):
        return rows_ref[128 * g : 128 * g + 128, 128 * m : 128 * m + 128]
    for g in range(8):
        for h in range(g, 8):
            m = h - g
            if m < 4:
                block = rows_of(g, m)
            elif m == 4:
                block = jnp.where(half_row == half_col, rows_of(g, 4), rows_of(h, 4).T)
            else:
                block = rows_of(h, 8 - m).T
            m_ref[128 * g : 128 * g + 128, 128 * h : 128 * h + 128] = block
            if m == 1 and g % 2 == 0:
                m_ref[128 * h : 128 * h + 128, 128 * g : 128 * g + 128] = block.T
        m_ref[128 * g : 128 * g + 128, ORDER : ORDER + 128] = panel_ref[:, 128 * g : 128 * g + 128].T
        spare = rows_of(g, 4)
        turned = pltpu.roll(spare, 64, axis=1)
        first_half = (half_row == 1) if g < 4 else (half_row == 0)
        right = jnp.where(first_half, spare, turned)
        m_ref[128 * g : 128 * g + 128, ORDER + 128 : full] = jnp.where((lane >= 3) & (lane < 6), right, 0.0)
    for k in range(STEPS):
        here = slice(WIDE * k, WIDE * (k + 1))
        later = WIDE * (k + 1)
        inv = split(inverse(m_ref[here, here]))
        values = product(inv, split(m_ref[here, later:full]))
        if k < STEPS - 1:
            high, low = split(values)
            vh_ref[here, later:full] = high
            vl_ref[here, later:full] = low
            for i in range(k + 1, STEPS):
                there = slice(WIDE * i, WIDE * (i + 1))
                left = split(m_ref[here, there].T)
                start = WIDE * (i - k - 1)
                m_ref[there, WIDE * i : full] -= product(left, (high[:, start:], low[:, start:]))
        else:
            out_ref[here, :] = values
    for k in range(STEPS - 2, -1, -1):
        here = slice(WIDE * k, WIDE * (k + 1))
        later = WIDE * (k + 1)
        own = vh_ref[here, ORDER:full].astype(F32) + vl_ref[here, ORDER:full].astype(F32)
        left = (vh_ref[here, later:ORDER], vl_ref[here, later:ORDER])
        out_ref[here, :] = own - product(left, split(out_ref[later:ORDER, :]))


def solve_system(rows, panel):
    full = ORDER + SIDE
    return pl.pallas_call(
        factor_body,
        out_shape=jax.ShapeDtypeStruct((ORDER, SIDE), F32),
        in_specs=[VMEM, VMEM],
        out_specs=VMEM,
        scratch_shapes=[
            pltpu.VMEM((ORDER, full), F32),
            pltpu.VMEM((ORDER, full), BF16),
            pltpu.VMEM((ORDER, full), BF16),
        ],
        compiler_params=pltpu.CompilerParams(vmem_limit_bytes=56 * 2**20),
        name="block_elimination",
    )(rows, panel)


SLOTS = 8
TILES = 64
RADIUS = 1.25
PHI_SCALE = 4.0 * 0.8**5
UNROLL = 2


def products_body(x_ref, rows_ref, trail_ref, out_ref, ctrl_ref):
    x_parts = split(x_ref[...])
    for c in range(8):
        here = slice(128 * c, 128 * c + 128)
        both = product(split(rows_ref[c, 0:128, :]), x_parts)
        out_ref[:, here] = trail_ref[:, here] - both[:, 0:128].T
        ctrl_ref[c] = rows_ref[c, 128:136, 0:128] - both[:, 128:256].T[0:8]


def apply_products(x, rows, trail):
    return pl.pallas_call(
        products_body,
        out_shape=(
            jax.ShapeDtypeStruct((128, 1024), F32),
            jax.ShapeDtypeStruct((8, 8, 128), F32),
        ),
        in_specs=[VMEM] * 3,
        out_specs=(VMEM, VMEM),
        compiler_params=pltpu.CompilerParams(vmem_limit_bytes=56 * 2**20),
        name="trail_and_weights",
    )(x, rows, trail)


def tile_sum(t, first_ref, count_ref, nodes_ref, ctrl_ref):
    here = pl.ds(pl.multiple_of(t * 128, 128), 128)
    first = first_ref[t]
    count = count_ref[t]
    spread = [
        jnp.broadcast_to(nodes_ref[a : a + 1, here], (128, 128)).T for a in range(3)
    ]
    highs, lows, weights = [], [], []
    for s in range(SLOTS):
        live = s < count
        block = jnp.where(live, first + s, first)
        ctrl = ctrl_ref[block % 32, block // 32]
        dist_sq = jnp.zeros((128, 128), F32)
        for a in range(3):
            differ = spread[a] - ctrl[a : a + 1, :]
            dist_sq = dist_sq + differ * differ
        dist = dist_sq * lax.rsqrt(jnp.maximum(dist_sq, 1e-30))
        remain = jnp.maximum(RADIUS - dist, 0.0)
        remain_sq = remain * remain
        phi = remain_sq * remain_sq * (RADIUS * RADIUS - remain)
        high, low = split(phi)
        highs.append(high)
        lows.append(low)
        w_high, w_low = split(jnp.where(live, ctrl, 0.0))
        weights.append(jnp.concatenate([w_high, w_low], axis=0))
    weight = jnp.concatenate(weights, axis=1)
    by_high = raw_dot(weight, jnp.concatenate(highs, axis=1), NT)
    by_low = raw_dot(weight, jnp.concatenate(lows, axis=1), NT)
    return (by_low[0:8] + by_high[8:16] + by_high[0:8]) * PHI_SCALE


def mesh_body(first_ref, count_ref, nodes_ref, ctrl_ref, area_ref, nbr_ref, old_ref, disp_ref, volume_ref, d_ref):
    def sums(i, carry):
        for u in range(UNROLL):
            t = i * UNROLL + u
            d_ref[t] = tile_sum(t, first_ref, count_ref, nodes_ref, ctrl_ref)
        return carry

    lax.fori_loop(0, (TILES + 2) // UNROLL, sums, 0)

    def fluxes(i, carry):
        for u in range(2):
            t = i * 2 + u
            here = pl.ds(pl.multiple_of(t * 128, 128), 128)
            index = nbr_ref[:, here] - t * 128
            which = index // 128
            lane = index - which * 128
            own = d_ref[t + 1]
            disp_ref[:, here] = own[3:6]
            low, high = d_ref[t], d_ref[t + 2]
            flux = jnp.zeros((6, 128), F32)
            for a in range(3):
                near = [
                    jnp.take_along_axis(
                        jnp.broadcast_to(v[3 + a : 4 + a], (6, 128)), lane, axis=1, mode="promise_in_bounds"
                    )
                    for v in (low, own, high)
                ]
                across = jnp.where(which == 0, near[0], jnp.where(which == 1, near[1], near[2]))
                flux = flux + area_ref[a, :, here] * (own[3 + a : 4 + a] + across)
            volume_ref[pl.ds(t, 1), :] = old_ref[pl.ds(t, 1), :] + 0.5 * jnp.sum(flux, axis=0, keepdims=True)
        return carry

    lax.fori_loop(0, TILES // 2, fluxes, 0)


def update_mesh(first, count, nodes, ctrl, area, nbr, old):
    SMEM = pl.BlockSpec(memory_space=pltpu.SMEM)
    return pl.pallas_call(
        mesh_body,
        out_shape=(
            jax.ShapeDtypeStruct((3, TILES * 128), F32),
            jax.ShapeDtypeStruct((TILES, 128), F32),
        ),
        in_specs=[SMEM, SMEM] + [VMEM] * 5,
        out_specs=(VMEM, VMEM),
        scratch_shapes=[pltpu.VMEM((TILES + 2, 8, 128), F32)],
        compiler_params=pltpu.CompilerParams(vmem_limit_bytes=56 * 2**20),
        name="rbf_and_flux",
    )(first, count, nodes, ctrl, area, nbr, old)


def pack_body(group_ref, diag_ref, rhs_diag_ref, panel_ref, xyz_ref, rhs_ref, rows_ref, send_ref):
    group = group_ref[0]
    part = group_ref[1]
    for m in range(5):
        column = lax.rem(group + m, 8) * 128
        rows_ref[:, 128 * m : 128 * m + 128] = diag_ref[:, pl.ds(pl.multiple_of(column, 128), 128)]
    tall = jnp.concatenate([jnp.zeros((3, 32), F32), rhs_diag_ref[...], jnp.zeros((2, 32), F32)], axis=0)
    wide = jnp.concatenate([tall, jnp.zeros((8, 96), F32)], axis=1)
    column = jnp.concatenate([wide, jnp.zeros((120, 128), F32)], axis=0).T[0:32]
    column = column + pltpu.roll(column, 64, axis=1)
    half = lax.broadcasted_iota(jnp.int32, (32, 128), 1) // 64
    kept = jnp.where(group < 4, part // 2, 1 - part // 2)
    rows_ref[:, 512:640] = jnp.where(half == kept, rows_ref[:, 512:640], column)
    send_ref[0:128, :] = panel_ref[...]
    send_ref[128:136, :] = jnp.zeros((8, 1024), F32)
    send_ref[128:131, 0:128] = xyz_ref[...]
    send_ref[131:134, 0:128] = rhs_ref[...]


def pack(place, diag, rhs_diag, panel, xyz, rhs):
    return pl.pallas_call(
        pack_body,
        out_shape=(jax.ShapeDtypeStruct((32, 640), F32), jax.ShapeDtypeStruct((136, 1024), F32)),
        in_specs=[pl.BlockSpec(memory_space=pltpu.SMEM)] + [VMEM] * 5,
        out_specs=(VMEM, VMEM),
        name="pack_rows",
    )(place, diag, rhs_diag, panel, xyz, rhs)


def to_all(block, axis):
    copies = jnp.broadcast_to(block[None], (lax.axis_size(axis),) + block.shape)
    return lax.all_to_all(copies, axis, 0, 0, tiled=True)


def per_device(
    diag_block,
    rhs_diag,
    panel_block,
    rhs_panel,
    trail,
    ctrl_xyz,
    node_xyz,
    tile_blocks,
    tile_count,
    face_area,
    edge_nbr,
    old_volume,
):
    place = lax.axis_index("vol")
    place = jnp.stack([place // 4, place % 4])
    rows, send = pack(place, diag_block, rhs_diag, panel_block, ctrl_xyz, rhs_panel)
    column_rows = lax.all_gather(send, "chol", axis=0, tiled=False)
    whole_rows = to_all(rows, "vol").reshape(1024, 640)

    def edge(tile):
        lists = jnp.stack([tile_blocks[tile, 0], tile_count[tile]]).astype(F32)
        xyz = node_xyz[:, -128:] if tile else node_xyz[:, :128]
        return jnp.concatenate([xyz, jnp.pad(lists[None], ((0, 4), (0, 126)))], axis=0)

    count = lax.axis_size("vol")
    forward = [(i, i + 1) for i in range(count - 1)]
    backward = [(i + 1, i) for i in range(count - 1)]
    low = lax.ppermute(edge(-1), "vol", forward)
    high = lax.ppermute(edge(0), "vol", backward)
    nodes = jnp.concatenate([low[0:3], node_xyz, high[0:3]], axis=1)
    firsts = jnp.concatenate([low[3, 0:1].astype(jnp.int32), tile_blocks[:, 0], high[3, 0:1].astype(jnp.int32)])
    counts = jnp.concatenate([low[3, 1:2].astype(jnp.int32), tile_count, high[3, 1:2].astype(jnp.int32)])

    x = solve_system(whole_rows, panel_block)
    trail_out, ctrl = apply_products(x, column_rows, trail)
    ctrl = to_all(ctrl, "vol")
    node_disp, new_volume = update_mesh(
        firsts, counts, nodes, ctrl, face_area, edge_nbr, old_volume.reshape(TILES, 128)
    )
    return (trail_out, node_disp, new_volume.reshape(-1))


def solution(mesh):
    return jax.shard_map(
        per_device,
        mesh=mesh,
        in_specs=(
            P("vol", None),
            P(None, "vol"),
            P(("chol", "vol"), None),
            P(None, ("chol", "vol")),
            P(("chol", "vol"), None),
            P(None, ("chol", "vol")),
            P(None, ("chol", "vol")),
            P(("chol", "vol"), None),
            P(("chol", "vol")),
            P(None, None, ("chol", "vol")),
            P(None, ("chol", "vol")),
            P(("chol", "vol")),
        ),
        out_specs=(P(("chol", "vol"), None), P(None, ("chol", "vol")), P(("chol", "vol"))),
        check_vma=False,
    )
```

time: 821 us -> 150 us (0.18)
  other arithmetic: 264 us -> 4.63 us
  local copies, waits for them, and re-layouts: 234 us -> 10.9 us
  blocking collectives: 162 us -> 0 us
  matrix products: 127 us -> 0 us
  Pallas kernels: 0 us -> 59.7 us
  waiting for transfers between devices: 3.17 us -> 35.9 us
  starting transfers between devices: 4.4 us -> 21.6 us
    another operation x33 -> x1, other arithmetic: 257 us -> 0.59 us  [per_device(): place = jnp.stack([place // 4, place % 4])]
    gather x18 -> x0, local copies, waits for them, and re-layouts: 190 us -> none  [the longest x2 180 us: per_device(): across_disp = extended[:, edge_nbr]]
    all_gather x3 -> x0, blocking collectives: 162 us -> none  [the longest x1 70.6 us: per_device(): lax.all_gather(ctrl_xyz, ('chol', 'vol'), axis=1, tiled=True)]
    dot_general x10 -> x0, matrix products: 90 us -> none  [the longest x8 84.3 us: slot_term(): jnp.einsum('tnc,atc->atn', kernel, near_weight, precision=highest_mode)]
    pallas_call x0 -> x4, Pallas kernels: none -> 59.7 us  [the longest x1 35.7 us: update_mesh(): pl.pallas_call(mesh_body, out_shape=(jax.ShapeDtypeStruct((3, TILES * 128...]
    another operation x44 -> x0, matrix products: 36.9 us -> none  [the longest x14 23.2 us: per_device(): factor = jnp.linalg.cholesky(whole_diag)]
    another operation x50 -> x0, local copies, waits for them, and re-layouts: 30.8 us -> none
    ppermute x2, waiting for transfers between devices: 2.45 us -> 20 us  [the longest x1 20 us: per_device(): high = lax.ppermute(edge(0), 'vol', backward)]
  transfers between devices with their start and end apart: 4 -> 5, of which waited for: 1 -> 2; matrix products, arithmetic and copies ran while one was open for 34% -> 7% of each run, Pallas kernels for 0% -> 11%
where the time goes in v1:
time: 150 us; the launch traced here: 149 us
  Pallas kernels  59.7 us (40%)
  waiting for transfers between devices  35.9 us (24%)
  starting transfers between devices  21.6 us (14%)
  between operations  16.7 us (11%)
  local copies, waits for them, and re-layouts  10.9 us (7%)
  other arithmetic  4.63 us (3%)
    pallas_call x1, Pallas kernels, update_mesh(): pl.pallas_call(mesh_body, out_shape=(jax.ShapeDtypeStruct((3, TILES * 128...  35.7 us
    ppermute x1, waiting for transfers between devices, per_device(): high = lax.ppermute(edge(0), 'vol', backward)  20 us
    pallas_call x1, Pallas kernels, solve_system(): pl.pallas_call(factor_body, out_shape=jax.ShapeDtypeStruct((ORDER, SIDE),...  16.6 us
    all_to_all x2, starting transfers between devices, to_all(): return lax.all_to_all(copies, axis, 0, 0, tiled=True)  16 us
    all_to_all x2, waiting for transfers between devices, to_all(): return lax.all_to_all(copies, axis, 0, 0, tiled=True)  15.9 us
    pallas_call x1, Pallas kernels, apply_products(): pl.pallas_call(products_body, out_shape=(jax.ShapeDtypeStruct((128, 1024)...  5.41 us
    broadcast_in_dim x2, local copies, waits for them, and re-layouts, to_all(): copies = jnp.broadcast_to(block[None], (lax.axis_size(axis),) + block.shape)  4.57 us
    ppermute x1, starting transfers between devices, per_device(): low = lax.ppermute(edge(-1), 'vol', forward)  3.42 us
  transfers between devices with their start and end apart: 5, of which 2 were waited for; matrix products, arithmetic and copies ran while one was open for 7% of the time, Pallas kernels for 11%

profile of v1, /device:TPU:1, one launch (start us, length us, event | category | flops | bytes accessed | tf_op | source)
XLA Modules:
  0.0 149.4 jit_solution(13706103622684457393)
XLA Ops:
  7.2 0.0 all-gather.3.cloned.1.call-start
  7.2 0.6 pad_add_fusion.group_ref
  7.8 2.1 %pack_rows.1 = (f32[32,640]{1,0:T(8,128)}, f32[136,1024]{1,0:T(8,128)}) custom-call(s32[2]{0:T(128)} %pad_add_fusion.group_ref, f32[32,1024]{1,0:T(8,128)} %diag_ref.1, f32[3,32]{1,0:T(4,128)} %rhs_diag_ref.1, f32[128,1024]{1,0:T(8,128)} %panel_ref.3, f32[3,128]{1,0:T(4,128)} %xyz_ref.1, f32[3,128]{1,0:T(4,128)} %rhs_ref.1), custom_call_target="tpu_custom_call" | custom-call | tf_op jit(solution)/shard_map/pack_rows/pallas_call | solution.py:272
  9.9 0.0 all-gather.3.cloned.1.call-update
  9.9 2.7 %broadcast_in_dim.4 = f32[32,32,640]{2,1,0:T(8,128)} broadcast(f32[32,640]{1,0:T(8,128)} %get-tuple-element.9), dimensions={1,2} | broadcast | bytes 2703360 | tf_op jit(solution)/shard_map/broadcast_in_dim | solution.py:282
  12.6 0.0 copy-start.3
  12.6 0.0 copy-start.2
  12.6 8.7 %all-to-all-start = ((f32[32,32,640]{2,1,0:T(8,128)}), f32[32,32,640]{2,1,0:T(8,128)S(1)}, u32[]{:S(2)}, u32[]{:S(2)}) async-start(f32[32,32,640]{2,1,0:T(8,128)} %broadcast_in_dim.4), calls=%async_computation | async-start | bytes 5242880 | tf_op jit(solution)/shard_map/all_to_all | solution.py:283
  21.3 0.0 copy-done.3
  21.3 0.6 fusion.4
  21.9 1.3 fusion.3
  23.3 1.3 add_convert_fusion.1
  24.6 0.0 copy-done.2
  24.6 2.1 %collective-permute-start.1 = (f32[8,128]{1,0:T(8,128)S(1)}, f32[8,128]{1,0:T(8,128)S(1)}, u32[]{:S(2)}, u32[]{:S(2)}) collective-permute-start(f32[8,128]{1,0:T(8,128)S(1)} %select_maximum_fusion), channel_id=1, source_target_pairs={{1,0},{2,1},{3,2},{4,3},{5,4},{6,5},{7,6},{8,7},{9,8},{10,9},{11,1... | collective-permute-start | bytes 12296 | tf_op jit(solution)/shard_map/ppermute | solution.py:315
  26.8 1.4 add_convert_fusion
  28.2 3.4 %collective-permute-start = (f32[8,128]{1,0:T(8,128)S(1)}, f32[8,128]{1,0:T(8,128)S(1)}, u32[]{:S(2)}, u32[]{:S(2)}) collective-permute-start(f32[8,128]{1,0:T(8,128)S(1)} %select_maximum_fusion.1), channel_id=1, source_target_pairs={{0,1},{1,2},{2,3},{3,4},{4,5},{5,6},{6,7},{7,8},{8,9},{9,10},{10,1... | collective-permute-start | bytes 12296 | tf_op jit(solution)/shard_map/ppermute | solution.py:314
  31.6 0.7 slice_bitcast_fusion
  32.3 20.0 %collective-permute-done.1 = f32[8,128]{1,0:T(8,128)S(1)} collective-permute-done((f32[8,128]{1,0:T(8,128)S(1)}, f32[8,128]{1,0:T(8,128)S(1)}, u32[]{:S(2)}, u32[]{:S(2)}) %collective-permute-start.1) | collective-permute-done | bytes 4128 | tf_op jit(solution)/shard_map/ppermute | solution.py:315
  52.3 0.6 fusion.2
  53.5 0.0 collective-permute-done
  53.5 0.6 fusion.1
  56.1 0.0 all-to-all-done
  56.1 0.0 copy-start
  56.1 1.5 %copy-done = f32[32,32,640]{2,1,0:T(8,128)} copy-done((f32[32,32,640]{2,1,0:T(8,128)}, f32[32,32,640]{2,1,0:T(8,128)S(1)}, u32[]{:S(2)}) %copy-start) | copy-done | bytes 2621464
  57.6 16.6 %block_elimination.1.x_ref = f32[1024,256]{1,0:T(8,128)} custom-call(f32[1024,640]{1,0:T(8,128)} %bitcast.16, f32[128,1024]{1,0:T(8,128)} %panel_ref.3), custom_call_target="tpu_custom_call" | custom-call | tf_op jit(solution)/shard_map/block_elimination/pallas_call | solution.py:125
  74.2 0.0 all-gather.3.cloned.1.call-done
  74.2 5.4 %trail_and_weights.1 = (f32[128,1024]{1,0:T(8,128)}, f32[8,8,128]{2,1,0:T(8,128)}) custom-call(f32[1024,256]{1,0:T(8,128)} %block_elimination.1.x_ref, f32[8,136,1024]{2,1,0:T(8,128)} %bitcast.17, f32[128,1024]{1,0:T(8,128)} %trail_ref.1), custom_call_target="tpu_custom_call" | custom-call | tf_op jit(solution)/shard_map/trail_and_weights/pallas_call | solution.py:157
  79.6 1.9 %broadcast_in_dim.5 = f32[32,8,8,128]{3,2,1,0:T(8,128)} broadcast(f32[8,8,128]{2,1,0:T(8,128)} %get-tuple-element.12), dimensions={1,2,3} | broadcast | bytes 1081344 | tf_op jit(solution)/shard_map/broadcast_in_dim | solution.py:282
  81.4 7.3 %all-to-all-start.1 = ((f32[32,8,8,128]{3,2,1,0:T(8,128)}), f32[32,8,8,128]{3,2,1,0:T(8,128)S(1)}, u32[]{:S(2)}, u32[]{:S(2)}) async-start(f32[32,8,8,128]{3,2,1,0:T(8,128)} %broadcast_in_dim.5), calls=%async_computation.1 | async-start | bytes 2097152 | tf_op jit(solution)/shard_map/all_to_all | solution.py:283
  88.7 0.6 pad_add_fusion.1
  89.3 0.7 pad_maximum_fusion.nodes_ref
  90.0 15.9 %all-to-all-done.1.ctrl_ref = f32[32,8,8,128]{3,2,1,0:T(8,128)S(1)} async-done(((f32[32,8,8,128]{3,2,1,0:T(8,128)}), f32[32,8,8,128]{3,2,1,0:T(8,128)S(1)}, u32[]{:S(2)}, u32[]{:S(2)}) %all-to-all-start.1) | async-done | bytes 1048608 | tf_op jit(solution)/shard_map/all_to_all | solution.py:283
  105.9 0.0 copy-start.1
  105.9 1.0 copy-done.1
  106.9 35.7 %rbf_and_flux.1 = (f32[3,8192]{1,0:T(4,128)}, f32[64,128]{1,0:T(8,128)}) custom-call(s32[66]{0:T(128)} %get-tuple-element.25.first_ref, s32[66]{0:T(128)} %get-tuple-element.26.count_ref, f32[3,8448]{1,0:T(4,128)} %pad_maximum_fusion.nodes_ref, f32[32,8,8,128]{3,2,1,0:T(8,128)} %copy-done.1, f32[3,6,8192]{2,1,0:T(8,128)} %area_ref.1, s32[6,8192]{1,0:T(8,128)} %nbr_ref.1, ...), custom_call_target="tpu_custom_call" | custom-call | tf_op jit(solution)/shard_map/rbf_and_flux/pallas_call | solution.py:238
  (5 shorter events, 0.0 us)
Async XLA Ops:
  7.2 67.0 %all-gather.3.cloned.1.call-start = ((), (), s32[]{:S(2)}) async-start(), calls=%async_computation.2 | async-start | bytes 5013504 | tf_op jit(solution)/shard_map/all_gather | solution.py:303
  12.6 8.7 %copy-start.3 = (s32[64]{0:T(128)S(1)}, s32[64]{0:T(128)}, u32[]{:S(2)}) copy-start(s32[64]{0:T(128)} %param.20) | copy-start | bytes 772
  12.6 12.0 %copy-start.2 = (f32[3,8192]{1,0:T(4,128)S(1)}, f32[3,8192]{1,0:T(4,128)}, u32[]{:S(2)}) copy-start(f32[3,8192]{1,0:T(4,128)} %param.18) | copy-start | bytes 294916
  12.6 43.5 %all-to-all-start = ((f32[32,32,640]{2,1,0:T(8,128)}), f32[32,32,640]{2,1,0:T(8,128)S(1)}, u32[]{:S(2)}, u32[]{:S(2)}) async-start(f32[32,32,640]{2,1,0:T(8,128)} %broadcast_in_dim.4), calls=%async_computation | async-start | bytes 5242880 | tf_op jit(solution)/shard_map/all_to_all | solution.py:283
  24.6 27.7 %collective-permute-start.1 = (f32[8,128]{1,0:T(8,128)S(1)}, f32[8,128]{1,0:T(8,128)S(1)}, u32[]{:S(2)}, u32[]{:S(2)}) collective-permute-start(f32[8,128]{1,0:T(8,128)S(1)} %select_maximum_fusion), channel_id=1, source_target_pairs={{1,0},{2,1},{3,2},{4,3},{5,4},{6,5},{7,6},{8,7},{9,8},{10,9},{11,1... | collective-permute-start | bytes 12296 | tf_op jit(solution)/shard_map/ppermute | solution.py:315
  28.2 25.4 %collective-permute-start = (f32[8,128]{1,0:T(8,128)S(1)}, f32[8,128]{1,0:T(8,128)S(1)}, u32[]{:S(2)}, u32[]{:S(2)}) collective-permute-start(f32[8,128]{1,0:T(8,128)S(1)} %select_maximum_fusion.1), channel_id=1, source_target_pairs={{0,1},{1,2},{2,3},{3,4},{4,5},{5,6},{6,7},{7,8},{8,9},{9,10},{10,1... | collective-permute-start | bytes 12296 | tf_op jit(solution)/shard_map/ppermute | solution.py:314
  56.1 1.5 %copy-start = (f32[32,32,640]{2,1,0:T(8,128)}, f32[32,32,640]{2,1,0:T(8,128)S(1)}, u32[]{:S(2)}) copy-start(f32[32,32,640]{2,1,0:T(8,128)S(1)} %all-to-all-done) | copy-start | bytes 7864324
  81.4 24.4 %all-to-all-start.1 = ((f32[32,8,8,128]{3,2,1,0:T(8,128)}), f32[32,8,8,128]{3,2,1,0:T(8,128)S(1)}, u32[]{:S(2)}, u32[]{:S(2)}) async-start(f32[32,8,8,128]{3,2,1,0:T(8,128)} %broadcast_in_dim.5), calls=%async_computation.1 | async-start | bytes 2097152 | tf_op jit(solution)/shard_map/all_to_all | solution.py:283
  105.9 1.0 copy-start.1
Sparse Core Ops, SparseCore 0:
  10.0 61.0 all-gather.2

commit v2 on v1

--- a/solution.py
+++ b/solution.py
@@ -11,9 +11,11 @@
 NT = (((1,), (1,)), ((), ()))
 WIDE = 256
 STEPS = 4
+CHIPS = 16
 ORDER = 1024
 SIDE = 256
 VMEM = pl.BlockSpec(memory_space=pltpu.VMEM)
+SMEM = pl.BlockSpec(memory_space=pltpu.SMEM)
 
 
 def split(value):
@@ -71,8 +73,12 @@
     return total / diag_row
 
 
-def factor_body(rows_ref, panel_ref, out_ref, m_ref, vh_ref, vl_ref):
+def factor_body(same_ref, other_ref, panel_ref, out_ref, rhs_ref, rows_ref, m_ref, vh_ref, vl_ref):
     full = ORDER + SIDE
+    core = lax.axis_index("vol") % 2
+    for i in range(16):
+        rows_ref[pl.ds(pl.multiple_of(64 * i + 32 * core, 32), 32), :] = same_ref[i]
+        rows_ref[pl.ds(pl.multiple_of(64 * i + 32 * (1 - core), 32), 32), :] = other_ref[i]
     half_row = lax.broadcasted_iota(jnp.int32, (128, 128), 0) // 64
     half_col = lax.broadcasted_iota(jnp.int32, (128, 128), 1) // 64
     lane = lax.broadcasted_iota(jnp.int32, (128, 128), 1)
@@ -118,57 +124,91 @@
         own = vh_ref[here, ORDER:full].astype(F32) + vl_ref[here, ORDER:full].astype(F32)
         left = (vh_ref[here, later:ORDER], vl_ref[here, later:ORDER])
         out_ref[here, :] = own - product(left, split(out_ref[later:ORDER, :]))
-
-
-def solve_system(rows, panel):
+    for g in range(8):
+        here = slice(128 * g, 128 * g + 128)
+        high, low = split(out_ref[here, 128:256].T[0:8])
+        rhs_ref[:, here] = jnp.concatenate([high, low], axis=0)
+
+
+def solve_system(same, other, panel):
     full = ORDER + SIDE
     return pl.pallas_call(
         factor_body,
-        out_shape=jax.ShapeDtypeStruct((ORDER, SIDE), F32),
-        in_specs=[VMEM, VMEM],
-        out_specs=VMEM,
+        out_shape=(jax.ShapeDtypeStruct((ORDER, SIDE), F32), jax.ShapeDtypeStruct((16, ORDER), BF16)),
+        in_specs=[VMEM] * 3,
+        out_specs=(VMEM, VMEM),
         scratch_shapes=[
+            pltpu.VMEM((ORDER, 640), F32),
             pltpu.VMEM((ORDER, full), F32),
             pltpu.VMEM((ORDER, full), BF16),
             pltpu.VMEM((ORDER, full), BF16),
         ],
         compiler_params=pltpu.CompilerParams(vmem_limit_bytes=56 * 2**20),
         name="block_elimination",
-    )(rows, panel)
+    )(same, other, panel)
 
 
 SLOTS = 8
 TILES = 64
 RADIUS = 1.25
 PHI_SCALE = 4.0 * 0.8**5
-UNROLL = 2
-
-
-def products_body(x_ref, rows_ref, trail_ref, out_ref, ctrl_ref):
-    x_parts = split(x_ref[...])
-    for c in range(8):
-        here = slice(128 * c, 128 * c + 128)
-        both = product(split(rows_ref[c, 0:128, :]), x_parts)
-        out_ref[:, here] = trail_ref[:, here] - both[:, 0:128].T
-        ctrl_ref[c] = rows_ref[c, 128:136, 0:128] - both[:, 128:256].T[0:8]
+UNROLL = 6
+
+
+def weights_body(rhs_ref, rows_ref, ctrl_ref):
+    for c in range(2):
+        high, low = split(rows_ref[c, 0:128, :])
+        by_high = raw_dot(rhs_ref[...], high, NT)
+        by_low = raw_dot(rhs_ref[...], low, NT)
+        ctrl = rows_ref[c, 128:136, 0:128] - (by_low[0:8] + by_high[8:16] + by_high[0:8])
+        ctrl_ref[:, c] = jnp.broadcast_to(ctrl, (CHIPS, 8, 128))
+
+
+def control_weights(rhs, rows):
+    return pl.pallas_call(
+        weights_body,
+        out_shape=jax.ShapeDtypeStruct((CHIPS, 8, 8, 128), F32),
+        grid=(4,),
+        in_specs=[
+            pl.BlockSpec((16, ORDER), lambda c: (0, 0)),
+            pl.BlockSpec((2, 136, ORDER), lambda c: (c, 0, 0)),
+        ],
+        out_specs=pl.BlockSpec((CHIPS, 2, 8, 128), lambda c: (0, c, 0, 0)),
+        compiler_params=pltpu.CompilerParams(vmem_limit_bytes=60 * 2**20),
+        name="control_weights",
+    )(rhs, rows)
+
+
+def products_body(x_ref, rows_ref, trail_ref, out_ref, high_ref, low_ref):
+    @pl.when(pl.program_id(0) == 0)
+    def _():
+        high_ref[...], low_ref[...] = split(x_ref[...])
+
+    sums = product(split(rows_ref[0, 0:128, :]), (high_ref[...], low_ref[...]))
+    out_ref[...] = trail_ref[...] - sums.T
 
 
 def apply_products(x, rows, trail):
     return pl.pallas_call(
         products_body,
-        out_shape=(
-            jax.ShapeDtypeStruct((128, 1024), F32),
-            jax.ShapeDtypeStruct((8, 8, 128), F32),
-        ),
-        in_specs=[VMEM] * 3,
-        out_specs=(VMEM, VMEM),
-        compiler_params=pltpu.CompilerParams(vmem_limit_bytes=56 * 2**20),
-        name="trail_and_weights",
+        out_shape=jax.ShapeDtypeStruct((128, ORDER), F32),
+        grid=(8,),
+        in_specs=[
+            pl.BlockSpec((ORDER, 128), lambda c: (0, 0)),
+            pl.BlockSpec((1, 136, ORDER), lambda c: (c, 0, 0)),
+            pl.BlockSpec((128, 128), lambda c: (0, c)),
+        ],
+        out_specs=pl.BlockSpec((128, 128), lambda c: (0, c)),
+        scratch_shapes=[pltpu.VMEM((ORDER, 128), BF16)] * 2,
+        compiler_params=pltpu.CompilerParams(vmem_limit_bytes=60 * 2**20),
+        cost_estimate=pl.CostEstimate(flops=3 * 2 * 128 * 1024 * 1024, bytes_accessed=6 * 2**20, transcendentals=0),
+        name="trail_update",
     )(x, rows, trail)
 
 
-def tile_sum(t, first_ref, count_ref, nodes_ref, ctrl_ref):
+def tile_sum(t, first_ref, count_ref, nodes_ref, same_ref, other_ref):
     here = pl.ds(pl.multiple_of(t * 128, 128), 128)
+    core = lax.axis_index("vol") % 2
     first = first_ref[t]
     count = count_ref[t]
     spread = [
@@ -178,7 +218,8 @@
     for s in range(SLOTS):
         live = s < count
         block = jnp.where(live, first + s, first)
-        ctrl = ctrl_ref[block % 32, block // 32]
+        chip, rank = (block // 2) % CHIPS, block // 32
+        ctrl = jnp.where(block % 2 == core, same_ref[chip, rank], other_ref[chip, rank])
         dist_sq = jnp.zeros((128, 128), F32)
         for a in range(3):
             differ = spread[a] - ctrl[a : a + 1, :]
@@ -198,18 +239,50 @@
     return (by_low[0:8] + by_high[8:16] + by_high[0:8]) * PHI_SCALE
 
 
-def mesh_body(first_ref, count_ref, nodes_ref, ctrl_ref, area_ref, nbr_ref, old_ref, disp_ref, volume_ref, d_ref):
+def mesh_body(
+    tile_first_ref,
+    tile_count_ref,
+    low_list_ref,
+    high_list_ref,
+    low_ref,
+    high_ref,
+    own_ref,
+    same_ref,
+    other_ref,
+    area_ref,
+    nbr_ref,
+    old_ref,
+    disp_ref,
+    volume_ref,
+    first_ref,
+    count_ref,
+    nodes_ref,
+    d_ref,
+):
+    def lists(t, carry):
+        first_ref[t + 1] = tile_first_ref[t]
+        count_ref[t + 1] = tile_count_ref[t]
+        return carry
+
+    lax.fori_loop(0, TILES, lists, 0)
+    for t, list_ref in ((0, low_list_ref), (TILES + 1, high_list_ref)):
+        first_ref[t] = list_ref[3, 0].astype(jnp.int32)
+        count_ref[t] = list_ref[3, 1].astype(jnp.int32)
+    nodes_ref[:, 0:128] = low_ref[0:3]
+    nodes_ref[:, 128 : 128 + TILES * 128] = own_ref[...]
+    nodes_ref[:, 128 + TILES * 128 :] = high_ref[0:3]
+
     def sums(i, carry):
         for u in range(UNROLL):
             t = i * UNROLL + u
-            d_ref[t] = tile_sum(t, first_ref, count_ref, nodes_ref, ctrl_ref)
+            d_ref[t] = tile_sum(t, first_ref, count_ref, nodes_ref, same_ref, other_ref)
         return carry
 
     lax.fori_loop(0, (TILES + 2) // UNROLL, sums, 0)
 
     def fluxes(i, carry):
-        for u in range(2):
-            t = i * 2 + u
+        for u in range(4):
+            t = i * 4 + u
             here = pl.ds(pl.multiple_of(t * 128, 128), 128)
             index = nbr_ref[:, here] - t * 128
             which = index // 128
@@ -230,57 +303,95 @@
             volume_ref[pl.ds(t, 1), :] = old_ref[pl.ds(t, 1), :] + 0.5 * jnp.sum(flux, axis=0, keepdims=True)
         return carry
 
-    lax.fori_loop(0, TILES // 2, fluxes, 0)
-
-
-def update_mesh(first, count, nodes, ctrl, area, nbr, old):
-    SMEM = pl.BlockSpec(memory_space=pltpu.SMEM)
+    lax.fori_loop(0, TILES // 4, fluxes, 0)
+
+
+def update_mesh(first, count, low, high, nodes, same, other, area, nbr, old):
     return pl.pallas_call(
         mesh_body,
         out_shape=(
             jax.ShapeDtypeStruct((3, TILES * 128), F32),
             jax.ShapeDtypeStruct((TILES, 128), F32),
         ),
-        in_specs=[SMEM, SMEM] + [VMEM] * 5,
+        in_specs=[SMEM] * 4 + [VMEM] * 8,
         out_specs=(VMEM, VMEM),
-        scratch_shapes=[pltpu.VMEM((TILES + 2, 8, 128), F32)],
+        scratch_shapes=[
+            pltpu.SMEM((TILES + 2,), jnp.int32),
+            pltpu.SMEM((TILES + 2,), jnp.int32),
+            pltpu.VMEM((3, (TILES + 2) * 128), F32),
+            pltpu.VMEM((TILES + 2, 8, 128), F32),
+        ],
         compiler_params=pltpu.CompilerParams(vmem_limit_bytes=56 * 2**20),
         name="rbf_and_flux",
-    )(first, count, nodes, ctrl, area, nbr, old)
-
-
-def pack_body(group_ref, diag_ref, rhs_diag_ref, panel_ref, xyz_ref, rhs_ref, rows_ref, send_ref):
-    group = group_ref[0]
-    part = group_ref[1]
-    for m in range(5):
+    )(first, count, low, high, low, high, nodes, same, other, area, nbr, old)
+
+
+def send_body(panel_ref, xyz_ref, rhs_ref, send_ref):
+    send_ref[0:128, :] = panel_ref[...]
+    send_ref[128:136, :] = jnp.zeros((8, 1024), F32)
+    send_ref[128:131, 0:128] = xyz_ref[...]
+    send_ref[131:134, 0:128] = rhs_ref[...]
+
+
+def pack_send(panel, xyz, rhs):
+    return pl.pallas_call(
+        send_body,
+        out_shape=jax.ShapeDtypeStruct((136, ORDER), F32),
+        in_specs=[VMEM] * 3,
+        out_specs=VMEM,
+        name="pack_panel",
+    )(panel, xyz, rhs)
+
+
+def pack_body(
+    first_ref, count_ref, diag_ref, rhs_diag_ref, nodes_ref, rows_ref, head_ref, tail_ref
+):
+    place = lax.axis_index("vol")
+    group, part = place // 4, place % 4
+    for m in range(4):
         column = lax.rem(group + m, 8) * 128
-        rows_ref[:, 128 * m : 128 * m + 128] = diag_ref[:, pl.ds(pl.multiple_of(column, 128), 128)]
+        value = diag_ref[:, pl.ds(pl.multiple_of(column, 128), 128)]
+        rows_ref[:, :, 128 * m : 128 * m + 128] = jnp.broadcast_to(value, (CHIPS, 32, 128))
     tall = jnp.concatenate([jnp.zeros((3, 32), F32), rhs_diag_ref[...], jnp.zeros((2, 32), F32)], axis=0)
     wide = jnp.concatenate([tall, jnp.zeros((8, 96), F32)], axis=1)
     column = jnp.concatenate([wide, jnp.zeros((120, 128), F32)], axis=0).T[0:32]
     column = column + pltpu.roll(column, 64, axis=1)
     half = lax.broadcasted_iota(jnp.int32, (32, 128), 1) // 64
     kept = jnp.where(group < 4, part // 2, 1 - part // 2)
-    rows_ref[:, 512:640] = jnp.where(half == kept, rows_ref[:, 512:640], column)
-    send_ref[0:128, :] = panel_ref[...]
-    send_ref[128:136, :] = jnp.zeros((8, 1024), F32)
-    send_ref[128:131, 0:128] = xyz_ref[...]
-    send_ref[131:134, 0:128] = rhs_ref[...]
-
-
-def pack(place, diag, rhs_diag, panel, xyz, rhs):
+    fifth = diag_ref[:, pl.ds(pl.multiple_of(lax.rem(group + 4, 8) * 128, 128), 128)]
+    rows_ref[:, :, 512:640] = jnp.broadcast_to(jnp.where(half == kept, fifth, column), (CHIPS, 32, 128))
+    row_id = lax.broadcasted_iota(jnp.int32, (8, 128), 0)
+    lane = lax.broadcasted_iota(jnp.int32, (8, 128), 1)
+    for edge_ref, tile in ((head_ref, 0), (tail_ref, TILES - 1)):
+        first = first_ref[tile].astype(F32)
+        count = count_ref[tile].astype(F32)
+        lists = jnp.where(lane == 0, first, jnp.where(lane == 1, count, 0.0))
+        edge_ref[...] = jnp.where(row_id == 3, lists, 0.0)
+        edge_ref[0:3, :] = nodes_ref[:, 128 * tile : 128 * tile + 128]
+
+
+def pack(first, count, diag, rhs_diag, nodes):
+    edge = jax.ShapeDtypeStruct((8, 128), F32)
     return pl.pallas_call(
         pack_body,
-        out_shape=(jax.ShapeDtypeStruct((32, 640), F32), jax.ShapeDtypeStruct((136, 1024), F32)),
-        in_specs=[pl.BlockSpec(memory_space=pltpu.SMEM)] + [VMEM] * 5,
-        out_specs=(VMEM, VMEM),
+        out_shape=(
+            jax.ShapeDtypeStruct((CHIPS, 32, 640), F32),
+            edge,
+            edge,
+        ),
+        in_specs=[SMEM] * 2 + [VMEM] * 3,
+        out_specs=(VMEM,) * 3,
         name="pack_rows",
-    )(place, diag, rhs_diag, panel, xyz, rhs)
-
-
-def to_all(block, axis):
-    copies = jnp.broadcast_to(block[None], (lax.axis_size(axis),) + block.shape)
-    return lax.all_to_all(copies, axis, 0, 0, tiled=True)
+    )(first, count, diag, rhs_diag, nodes)
+
+
+def chips_to_all(copies):
+    groups = [[2 * i + core for i in range(CHIPS)] for core in range(2)]
+    return lax.all_to_all(copies, "vol", 0, 0, tiled=True, axis_index_groups=groups)
+
+
+def other_core(blocks):
+    return lax.ppermute(blocks, "vol", [(i, i ^ 1) for i in range(2 * CHIPS)])
 
 
 def per_device(
@@ -297,31 +408,22 @@
     edge_nbr,
     old_volume,
 ):
-    place = lax.axis_index("vol")
-    place = jnp.stack([place // 4, place % 4])
-    rows, send = pack(place, diag_block, rhs_diag, panel_block, ctrl_xyz, rhs_panel)
-    column_rows = lax.all_gather(send, "chol", axis=0, tiled=False)
-    whole_rows = to_all(rows, "vol").reshape(1024, 640)
-
-    def edge(tile):
-        lists = jnp.stack([tile_blocks[tile, 0], tile_count[tile]]).astype(F32)
-        xyz = node_xyz[:, -128:] if tile else node_xyz[:, :128]
-        return jnp.concatenate([xyz, jnp.pad(lists[None], ((0, 4), (0, 126)))], axis=0)
-
-    count = lax.axis_size("vol")
-    forward = [(i, i + 1) for i in range(count - 1)]
-    backward = [(i + 1, i) for i in range(count - 1)]
-    low = lax.ppermute(edge(-1), "vol", forward)
-    high = lax.ppermute(edge(0), "vol", backward)
-    nodes = jnp.concatenate([low[0:3], node_xyz, high[0:3]], axis=1)
-    firsts = jnp.concatenate([low[3, 0:1].astype(jnp.int32), tile_blocks[:, 0], high[3, 0:1].astype(jnp.int32)])
-    counts = jnp.concatenate([low[3, 1:2].astype(jnp.int32), tile_count, high[3, 1:2].astype(jnp.int32)])
-
-    x = solve_system(whole_rows, panel_block)
-    trail_out, ctrl = apply_products(x, column_rows, trail)
-    ctrl = to_all(ctrl, "vol")
+    firsts = tile_blocks[:, 0]
+    rows, head, tail = pack(firsts, tile_count, diag_block, rhs_diag, node_xyz)
+    column_rows = lax.all_gather(pack_send(panel_block, ctrl_xyz, rhs_panel), "chol", axis=0, tiled=False)
+    same_rows = chips_to_all(rows)
+    other_rows = other_core(same_rows)
+    size = lax.axis_size("vol")
+    low = lax.ppermute(tail, "vol", [(i, i + 1) for i in range(size - 1)])
+    high = lax.ppermute(head, "vol", [(i + 1, i) for i in range(size - 1)])
+    other_rows, low, high = lax.optimization_barrier((other_rows, low, high))
+    x, rhs_solved = solve_system(same_rows, other_rows, panel_block)
+    same_ctrl = chips_to_all(control_weights(rhs_solved, column_rows))
+    trail_out = apply_products(x, column_rows, trail)
+    same_ctrl, trail_out = lax.optimization_barrier((same_ctrl, trail_out))
+    other_ctrl = other_core(same_ctrl)
     node_disp, new_volume = update_mesh(
-        firsts, counts, nodes, ctrl, face_area, edge_nbr, old_volume.reshape(TILES, 128)
+        firsts, tile_count, low, high, node_xyz, same_ctrl, other_ctrl, face_area, edge_nbr, old_volume.reshape(TILES, 128)
     )
     return (trail_out, node_disp, new_volume.reshape(-1))
 

time: 150 us -> 135 us (0.900)
  blocking collectives: 0 us -> 26.8 us
  waiting for transfers between devices: 35.9 us -> 11.5 us
  local copies, waits for them, and re-layouts: 10.9 us -> 3.18 us
  starting transfers between devices: 21.6 us -> 14.7 us
  Pallas kernels: 59.7 us -> 64.5 us
  other arithmetic: 4.63 us -> 0 us
  between operations: 16.7 us -> 14.1 us
    all_to_all x0 -> x1, blocking collectives: none -> 26.8 us  [chips_to_all(): lax.all_to_all(copies, 'vol', 0, 0, tiled=True, axis_index_groups=groups)]
    ppermute x2 -> x4, waiting for transfers between devices: 20 us -> 4.61 us  [the longest x1 3.07 us: per_device(): high = lax.ppermute(head, 'vol', [(i + 1, i) for i in range(size - 1)])]
    all_to_all x2 -> x1, waiting for transfers between devices: 15.9 us -> 2.84 us  [chips_to_all(): lax.all_to_all(copies, 'vol', 0, 0, tiled=True, axis_index_groups=groups)]
    pallas_call x3 -> x5, Pallas kernels: 24 us -> 33.6 us  [the longest x1 17 us: solve_system(): pl.pallas_call(factor_body, out_shape=(jax.ShapeDtypeStruct((ORDER, SIDE)...]
    all_to_all x2 -> x1, starting transfers between devices: 16 us -> 6.53 us  [chips_to_all(): lax.all_to_all(copies, 'vol', 0, 0, tiled=True, axis_index_groups=groups)]
    pallas_call x1, Pallas kernels: 35.7 us -> 30.9 us  [update_mesh(): pl.pallas_call(mesh_body, out_shape=(jax.ShapeDtypeStruct((3, TILES * 128...]
    broadcast_in_dim x2 -> x0, local copies, waits for them, and re-layouts: 4.57 us -> none  [to_all(): copies = jnp.broadcast_to(block[None], (lax.axis_size(axis),) + block.shape)]
    all_gather x1, waiting for transfers between devices: 0.01 us -> 3.99 us  [per_device(): lax.all_gather(pack_send(panel_block, ctrl_xyz, rhs_panel), 'chol', axis=...]
  transfers between devices with their start and end apart: 5 -> 6, of which waited for: 2 -> 4; matrix products, arithmetic and copies ran while one was open for 7% -> 1% of each run, Pallas kernels for 11% -> 20%
where the time goes in v2:
time: 135 us
  Pallas kernels  64.5 us (48%)
  blocking collectives  26.8 us (20%)
  starting transfers between devices  14.7 us (11%)
  between operations  14.1 us (10%)
  waiting for transfers between devices  11.5 us (9%)
  local copies, waits for them, and re-layouts  3.18 us (2%)
    pallas_call x1, Pallas kernels, update_mesh(): pl.pallas_call(mesh_body, out_shape=(jax.ShapeDtypeStruct((3, TILES * 128...  30.9 us
    all_to_all x1, blocking collectives, chips_to_all(): lax.all_to_all(copies, 'vol', 0, 0, tiled=True, axis_index_groups=groups)  26.8 us
    pallas_call x1, Pallas kernels, solve_system(): pl.pallas_call(factor_body, out_shape=(jax.ShapeDtypeStruct((ORDER, SIDE)...  17 us
    pallas_call x1, Pallas kernels, apply_products(): pl.pallas_call(products_body, out_shape=jax.ShapeDtypeStruct((128, ORDER)...  7.67 us
    all_to_all x1, starting transfers between devices, chips_to_all(): lax.all_to_all(copies, 'vol', 0, 0, tiled=True, axis_index_groups=groups)  6.53 us
    pallas_call x1, Pallas kernels, control_weights(): pl.pallas_call(weights_body, out_shape=jax.ShapeDtypeStruct((CHIPS, 8, 8,...  4.7 us
    all_gather x1, waiting for transfers between devices, per_device(): lax.all_gather(pack_send(panel_block, ctrl_xyz, rhs_panel), 'chol', axis=...  3.99 us
    ppermute x2, starting transfers between devices, other_core(): return lax.ppermute(blocks, 'vol', [(i, i ^ 1) for i in range(2 * CHIPS)])  3.78 us
  transfers between devices with their start and end apart: 6, of which 4 were waited for; matrix products, arithmetic and copies ran while one was open for 1% of the time, Pallas kernels for 20%

profile of v2, /device:TPU:1, one launch (start us, length us, event | category | flops | bytes accessed | tf_op | source)
XLA Modules:
  0.0 134.7 jit_solution(274160185352928465)
XLA Ops:
  7.2 0.0 all-gather.3.cloned.1.call-start
  7.2 1.9 %pack_panel.1 = f32[136,1024]{1,0:T(8,128)} custom-call(f32[128,1024]{1,0:T(8,128)} %panel_ref.3, f32[3,128]{1,0:T(4,128)} %xyz_ref.1, f32[3,128]{1,0:T(4,128)} %rhs_ref.1), custom_call_target="tpu_custom_call" | custom-call | tf_op jit(solution)/shard_map/pack_panel/pallas_call | solution.py:337
  9.2 0.0 all-gather.3.cloned.1.call-update
  9.2 1.3 slice_bitcast_fusion.first_ref.tile_first_ref
  10.5 2.3 %pack_rows.1 = (f32[16,32,640]{2,1,0:T(8,128)}, f32[8,128]{1,0:T(8,128)}, f32[8,128]{1,0:T(8,128)}) custom-call(s32[64]{0:T(128)} %slice_bitcast_fusion.first_ref.tile_first_ref, s32[64]{0:T(128)} %tile_count_ref.1, f32[32,1024]{1,0:T(8,128)} %diag_ref.1, f32[3,32]{1,0:T(4,128)} %rhs_diag_ref.1, f32[3,8192]{1,0:T(4,128)} %own_ref.1), custom_call_target="tpu_custom_call" | custom-call | tf_op jit(solution)/shard_map/pack_rows/pallas_call | solution.py:375
  12.8 0.0 copy-start.7
  12.8 0.0 copy-start.6
  12.8 26.8 %all_to_all.10.same_ref = f32[16,32,640]{2,1,0:T(8,128)S(1)} all-to-all(f32[16,32,640]{2,1,0:T(8,128)} %get-tuple-element.15), channel_id=1, replica_groups={{0,2,4,6,8,10,12,14,16,18,20,22,24,26,28,30},{1,3,5,7,9,11,13,15,17,19,..., dimensions={0} | all-to-all | bytes 2621440 | tf_op jit(solution)/shard_map/all_to_all | solution.py:390
  39.6 0.0 copy-start
  39.6 1.8 %collective-permute-start = (f32[16,32,640]{2,1,0:T(8,128)S(1)}, f32[16,32,640]{2,1,0:T(8,128)S(1)}, u32[]{:S(2)}, u32[]{:S(2)}) collective-permute-start(f32[16,32,640]{2,1,0:T(8,128)S(1)} %all_to_all.10.same_ref), channel_id=1, source_target_pairs={{0,1},{1,0},{2,3},{3,2},{4,5},{5,4},{6,7},{7,6},{8,9},{9,8},{10,11... | collective-permute-start | bytes 3932168 | tf_op jit(solution)/shard_map/ppermute | solution.py:394
  41.4 0.0 copy-done.7
  41.4 2.1 %collective-permute-start.1 = (f32[8,128]{1,0:T(8,128)S(1)}, f32[8,128]{1,0:T(8,128)S(1)}, u32[]{:S(2)}, u32[]{:S(2)}) collective-permute-start(f32[8,128]{1,0:T(8,128)S(1)} %copy-done.7), channel_id=1, source_target_pairs={{0,1},{1,2},{2,3},{3,4},{4,5},{5,6},{6,7},{7,8},{8,9},{9,10},{10,1... | collective-permute-start | bytes 12296 | tf_op jit(solution)/shard_map/ppermute | solution.py:417
  43.5 0.0 copy-done.6
  43.5 2.2 %collective-permute-start.2 = (f32[8,128]{1,0:T(8,128)S(1)}, f32[8,128]{1,0:T(8,128)S(1)}, u32[]{:S(2)}, u32[]{:S(2)}) collective-permute-start(f32[8,128]{1,0:T(8,128)S(1)} %copy-done.6), channel_id=1, source_target_pairs={{1,0},{2,1},{3,2},{4,3},{5,4},{6,5},{7,6},{8,7},{9,8},{10,9},{11,1... | collective-permute-start | bytes 12296 | tf_op jit(solution)/shard_map/ppermute | solution.py:418
  45.7 0.0 collective-permute-done.1.low_list_ref.low_ref
  45.7 0.0 copy-start.4
  45.8 3.1 %collective-permute-done.2.high_list_ref.high_ref = f32[8,128]{1,0:T(8,128)S(1)} collective-permute-done((f32[8,128]{1,0:T(8,128)S(1)}, f32[8,128]{1,0:T(8,128)S(1)}, u32[]{:S(2)}, u32[]{:S(2)}) %collective-permute-start.2) | collective-permute-done | bytes 4128 | tf_op jit(solution)/shard_map/ppermute | solution.py:418
  48.8 0.0 copy-start.5
  48.8 0.0 collective-permute-done.other_ref
  48.8 0.0 copy-done
  48.8 0.0 copy-start.2
  48.8 1.1 copy-done.2
  49.9 17.0 %block_elimination.1 = (f32[1024,256]{1,0:T(8,128)}, bf16[16,1024]{1,0:T(8,128)(2,1)}) custom-call(f32[16,32,640]{2,1,0:T(8,128)} %copy-done, f32[16,32,640]{2,1,0:T(8,128)} %copy-done.2, f32[128,1024]{1,0:T(8,128)} %panel_ref.3), custom_call_target="tpu_custom_call" | custom-call | tf_op jit(solution)/shard_map/block_elimination/pallas_call | solution.py:135
  66.9 4.0 %all-gather.3.cloned.1.call-done = f32[1088,1024]{1,0:T(8,128)} async-done(((f32[136,1024]{1,0:T(8,128)}), f32[1088,1024]{1,0:T(8,128)}) %all-gather.3.cloned.1.call-update) | async-done | bytes 4456464 | tf_op jit(solution)/shard_map/all_gather | solution.py:413
  70.9 4.7 %control_weights.1 = f32[16,8,8,128]{3,2,1,0:T(8,128)} custom-call(bf16[16,1024]{1,0:T(8,128)(2,1)} %get-tuple-element.19.rhs_ref, f32[8,136,1024]{2,1,0:T(8,128)} %bitcast.5), custom_call_target="tpu_custom_call" | custom-call | tf_op jit(solution)/shard_map/control_weights/pallas_call | solution.py:168
  75.6 0.0 copy-done.4
  75.6 0.0 copy-done.5
  75.6 6.5 %all-to-all-start.1 = ((f32[16,8,8,128]{3,2,1,0:T(8,128)}), f32[16,8,8,128]{3,2,1,0:T(8,128)S(1)}, u32[]{:S(2)}, u32[]{:S(2)}) async-start(f32[16,8,8,128]{3,2,1,0:T(8,128)} %control_weights.1), calls=%async_computation.1 | async-start | bytes 1048576 | tf_op jit(solution)/shard_map/all_to_all | solution.py:390
  82.1 7.7 %trail_update.1 = f32[128,1024]{1,0:T(8,128)} custom-call(f32[1024,256]{1,0:T(8,128)} %get-tuple-element.20.x_ref, f32[8,136,1024]{2,1,0:T(8,128)} %bitcast.6, f32[128,1024]{1,0:T(8,128)} %trail_ref.1), custom_call_target="tpu_custom_call" | custom-call | flops 805306368 | bytes 6291456 | tf_op jit(solution)/shard_map/trail_update/pallas_call | solution.py:192
  89.8 2.8 %all-to-all-done.1.same_ref = f32[16,8,8,128]{3,2,1,0:T(8,128)S(1)} async-done(((f32[16,8,8,128]{3,2,1,0:T(8,128)}), f32[16,8,8,128]{3,2,1,0:T(8,128)S(1)}, u32[]{:S(2)}, u32[]{:S(2)}) %all-to-all-start.1) | async-done | bytes 524320 | tf_op jit(solution)/shard_map/all_to_all | solution.py:390
  92.7 0.0 copy-start.1
  92.7 2.0 %collective-permute-start.3 = (f32[16,8,8,128]{3,2,1,0:T(8,128)S(1)}, f32[16,8,8,128]{3,2,1,0:T(8,128)S(1)}, u32[]{:S(2)}, u32[]{:S(2)}) collective-permute-start(f32[16,8,8,128]{3,2,1,0:T(8,128)S(1)} %all-to-all-done.1.same_ref), channel_id=1, source_target_pairs={{0,1},{1,0},{2,3},{3,2},{4,5},{5,4},{6,7},{7,6},{8,9},{9,8},{10,11... | collective-permute-start | bytes 1572872 | tf_op jit(solution)/shard_map/ppermute | solution.py:394
  94.6 1.5 %collective-permute-done.3.other_ref = f32[16,8,8,128]{3,2,1,0:T(8,128)S(1)} collective-permute-done((f32[16,8,8,128]{3,2,1,0:T(8,128)S(1)}, f32[16,8,8,128]{3,2,1,0:T(8,128)S(1)}, u32[]{:S(2)}, u32[]{:S(2)}) %collective-permute-start.3) | collective-permute-done | bytes 524320 | tf_op jit(solution)/shard_map/ppermute | solution.py:394
  96.2 0.0 copy-start.3
  96.2 0.0 copy-done.1
  96.2 0.8 copy-done.3
  97.0 30.9 %rbf_and_flux.1 = (f32[3,8192]{1,0:T(4,128)}, f32[64,128]{1,0:T(8,128)}) custom-call(s32[64]{0:T(128)} %slice_bitcast_fusion.first_ref.tile_first_ref, s32[64]{0:T(128)} %tile_count_ref.1, f32[8,128]{1,0:T(8,128)} %copy-done.4, f32[8,128]{1,0:T(8,128)} %copy-done.5, f32[8,128]{1,0:T(8,128)} %copy-done.4, f32[8,128]{1,0:T(8,128)} %copy-done.5, ...), custom_call_target="tpu_custom_call" | custom-call | tf_op jit(solution)/shard_map/rbf_and_flux/pallas_call | solution.py:310
Async XLA Ops:
  7.2 63.7 %all-gather.3.cloned.1.call-start = ((), (), s32[]{:S(2)}) async-start(), calls=%async_computation.2 | async-start | bytes 5013504 | tf_op jit(solution)/shard_map/all_gather | solution.py:413
  12.8 28.6 %copy-start.7 = (f32[8,128]{1,0:T(8,128)S(1)}, f32[8,128]{1,0:T(8,128)}, u32[]{:S(2)}) copy-start(f32[8,128]{1,0:T(8,128)} %get-tuple-element.16) | copy-start | bytes 12292
  12.8 30.7 %copy-start.6 = (f32[8,128]{1,0:T(8,128)S(1)}, f32[8,128]{1,0:T(8,128)}, u32[]{:S(2)}) copy-start(f32[8,128]{1,0:T(8,128)} %get-tuple-element.17) | copy-start | bytes 12292
  39.6 9.2 %copy-start = (f32[16,32,640]{2,1,0:T(8,128)}, f32[16,32,640]{2,1,0:T(8,128)S(1)}, u32[]{:S(2)}) copy-start(f32[16,32,640]{2,1,0:T(8,128)S(1)} %all_to_all.10.same_ref) | copy-start | bytes 3932164
  39.6 9.2 %collective-permute-start = (f32[16,32,640]{2,1,0:T(8,128)S(1)}, f32[16,32,640]{2,1,0:T(8,128)S(1)}, u32[]{:S(2)}, u32[]{:S(2)}) collective-permute-start(f32[16,32,640]{2,1,0:T(8,128)S(1)} %all_to_all.10.same_ref), channel_id=1, source_target_pairs={{0,1},{1,0},{2,3},{3,2},{4,5},{5,4},{6,7},{7,6},{8,9},{9,8},{10,11... | collective-permute-start | bytes 3932168 | tf_op jit(solution)/shard_map/ppermute | solution.py:394
  41.4 4.3 %collective-permute-start.1 = (f32[8,128]{1,0:T(8,128)S(1)}, f32[8,128]{1,0:T(8,128)S(1)}, u32[]{:S(2)}, u32[]{:S(2)}) collective-permute-start(f32[8,128]{1,0:T(8,128)S(1)} %copy-done.7), channel_id=1, source_target_pairs={{0,1},{1,2},{2,3},{3,4},{4,5},{5,6},{6,7},{7,8},{8,9},{9,10},{10,1... | collective-permute-start | bytes 12296 | tf_op jit(solution)/shard_map/ppermute | solution.py:417
  43.5 5.3 %collective-permute-start.2 = (f32[8,128]{1,0:T(8,128)S(1)}, f32[8,128]{1,0:T(8,128)S(1)}, u32[]{:S(2)}, u32[]{:S(2)}) collective-permute-start(f32[8,128]{1,0:T(8,128)S(1)} %copy-done.6), channel_id=1, source_target_pairs={{1,0},{2,1},{3,2},{4,3},{5,4},{6,5},{7,6},{8,7},{9,8},{10,9},{11,1... | collective-permute-start | bytes 12296 | tf_op jit(solution)/shard_map/ppermute | solution.py:418
  45.7 29.9 %copy-start.4 = (f32[8,128]{1,0:T(8,128)}, f32[8,128]{1,0:T(8,128)S(1)}, u32[]{:S(2)}) copy-start(f32[8,128]{1,0:T(8,128)S(1)} %collective-permute-done.1.low_list_ref.low_ref) | copy-start | bytes 12292
  48.8 26.8 %copy-start.5 = (f32[8,128]{1,0:T(8,128)}, f32[8,128]{1,0:T(8,128)S(1)}, u32[]{:S(2)}) copy-start(f32[8,128]{1,0:T(8,128)S(1)} %collective-permute-done.2.high_list_ref.high_ref) | copy-start | bytes 12292
  48.8 1.1 copy-start.2
  75.6 17.0 %all-to-all-start.1 = ((f32[16,8,8,128]{3,2,1,0:T(8,128)}), f32[16,8,8,128]{3,2,1,0:T(8,128)S(1)}, u32[]{:S(2)}, u32[]{:S(2)}) async-start(f32[16,8,8,128]{3,2,1,0:T(8,128)} %control_weights.1), calls=%async_computation.1 | async-start | bytes 1048576 | tf_op jit(solution)/shard_map/all_to_all | solution.py:390
  92.7 3.5 %copy-start.1 = (f32[16,8,8,128]{3,2,1,0:T(8,128)}, f32[16,8,8,128]{3,2,1,0:T(8,128)S(1)}, u32[]{:S(2)}) copy-start(f32[16,8,8,128]{3,2,1,0:T(8,128)S(1)} %all-to-all-done.1.same_ref) | copy-start | bytes 1572868
  92.7 3.5 %collective-permute-start.3 = (f32[16,8,8,128]{3,2,1,0:T(8,128)S(1)}, f32[16,8,8,128]{3,2,1,0:T(8,128)S(1)}, u32[]{:S(2)}, u32[]{:S(2)}) collective-permute-start(f32[16,8,8,128]{3,2,1,0:T(8,128)S(1)} %all-to-all-done.1.same_ref), channel_id=1, source_target_pairs={{0,1},{1,0},{2,3},{3,2},{4,5},{5,4},{6,7},{7,6},{8,9},{9,8},{10,11... | collective-permute-start | bytes 1572872 | tf_op jit(solution)/shard_map/ppermute | solution.py:394
  96.2 0.8 copy-start.3
Sparse Core Ops, SparseCore 0:
  9.8 61.0 all-gather.2

commit v3 on v2

--- a/solution.py
+++ b/solution.py
@@ -16,6 +16,7 @@
 SIDE = 256
 VMEM = pl.BlockSpec(memory_space=pltpu.VMEM)
 SMEM = pl.BlockSpec(memory_space=pltpu.SMEM)
+ANY = pl.BlockSpec(memory_space=pl.ANY)
 
 
 def split(value):
@@ -152,11 +153,11 @@
 TILES = 64
 RADIUS = 1.25
 PHI_SCALE = 4.0 * 0.8**5
-UNROLL = 6
+UNROLL = 11
 
 
 def weights_body(rhs_ref, rows_ref, ctrl_ref):
-    for c in range(2):
+    for c in range(4):
         high, low = split(rows_ref[c, 0:128, :])
         by_high = raw_dot(rhs_ref[...], high, NT)
         by_low = raw_dot(rhs_ref[...], low, NT)
@@ -168,12 +169,12 @@
     return pl.pallas_call(
         weights_body,
         out_shape=jax.ShapeDtypeStruct((CHIPS, 8, 8, 128), F32),
-        grid=(4,),
+        grid=(2,),
         in_specs=[
             pl.BlockSpec((16, ORDER), lambda c: (0, 0)),
-            pl.BlockSpec((2, 136, ORDER), lambda c: (c, 0, 0)),
+            pl.BlockSpec((4, 136, ORDER), lambda c: (c, 0, 0)),
         ],
-        out_specs=pl.BlockSpec((CHIPS, 2, 8, 128), lambda c: (0, c, 0, 0)),
+        out_specs=pl.BlockSpec((CHIPS, 4, 8, 128), lambda c: (0, c, 0, 0)),
         compiler_params=pltpu.CompilerParams(vmem_limit_bytes=60 * 2**20),
         name="control_weights",
     )(rhs, rows)
@@ -247,8 +248,8 @@
     low_ref,
     high_ref,
     own_ref,
-    same_ref,
-    other_ref,
+    same_any,
+    other_any,
     area_ref,
     nbr_ref,
     old_ref,
@@ -258,7 +259,17 @@
     count_ref,
     nodes_ref,
     d_ref,
+    same_ref,
+    other_ref,
+    sems,
 ):
+    copies = [
+        pltpu.make_async_copy(same_any, same_ref, sems.at[0]),
+        pltpu.make_async_copy(other_any, other_ref, sems.at[1]),
+    ]
+    for copy in copies:
+        copy.start()
+
     def lists(t, carry):
         first_ref[t + 1] = tile_first_ref[t]
         count_ref[t + 1] = tile_count_ref[t]
@@ -272,38 +283,39 @@
     nodes_ref[:, 128 : 128 + TILES * 128] = own_ref[...]
     nodes_ref[:, 128 + TILES * 128 :] = high_ref[0:3]
 
+    def flux_tile(t):
+        here = pl.ds(pl.multiple_of(t * 128, 128), 128)
+        index = nbr_ref[:, here] - t * 128
+        which = index // 128
+        lane = index - which * 128
+        low, own, high = d_ref[t], d_ref[t + 1], d_ref[t + 2]
+        disp_ref[:, here] = own[3:6]
+        flux = jnp.zeros((6, 128), F32)
+        for a in range(3):
+            near = [
+                jnp.take_along_axis(
+                    jnp.broadcast_to(v[3 + a : 4 + a], (6, 128)), lane, axis=1, mode="promise_in_bounds"
+                )
+                for v in (low, own, high)
+            ]
+            across = jnp.where(which == 0, near[0], jnp.where(which == 1, near[1], near[2]))
+            flux = flux + area_ref[a, :, here] * (own[3 + a : 4 + a] + across)
+        volume_ref[pl.ds(t, 1), :] = old_ref[pl.ds(t, 1), :] + 0.5 * jnp.sum(flux, axis=0, keepdims=True)
+
     def sums(i, carry):
+        for u in range(UNROLL):
+            flux_tile(jnp.maximum((i - 1) * UNROLL + u - 2, 0))
         for u in range(UNROLL):
             t = i * UNROLL + u
             d_ref[t] = tile_sum(t, first_ref, count_ref, nodes_ref, same_ref, other_ref)
         return carry
 
+    d_ref[0:3] = jnp.zeros((3, 8, 128), F32)
+    for copy in copies:
+        copy.wait()
     lax.fori_loop(0, (TILES + 2) // UNROLL, sums, 0)
-
-    def fluxes(i, carry):
-        for u in range(4):
-            t = i * 4 + u
-            here = pl.ds(pl.multiple_of(t * 128, 128), 128)
-            index = nbr_ref[:, here] - t * 128
-            which = index // 128
-            lane = index - which * 128
-            own = d_ref[t + 1]
-            disp_ref[:, here] = own[3:6]
-            low, high = d_ref[t], d_ref[t + 2]
-            flux = jnp.zeros((6, 128), F32)
-            for a in range(3):
-                near = [
-                    jnp.take_along_axis(
-                        jnp.broadcast_to(v[3 + a : 4 + a], (6, 128)), lane, axis=1, mode="promise_in_bounds"
-                    )
-                    for v in (low, own, high)
-                ]
-                across = jnp.where(which == 0, near[0], jnp.where(which == 1, near[1], near[2]))
-                flux = flux + area_ref[a, :, here] * (own[3 + a : 4 + a] + across)
-            volume_ref[pl.ds(t, 1), :] = old_ref[pl.ds(t, 1), :] + 0.5 * jnp.sum(flux, axis=0, keepdims=True)
-        return carry
-
-    lax.fori_loop(0, TILES // 4, fluxes, 0)
+    for u in range(UNROLL):
+        flux_tile(TILES - UNROLL + u)
 
 
 def update_mesh(first, count, low, high, nodes, same, other, area, nbr, old):
@@ -313,32 +325,47 @@
             jax.ShapeDtypeStruct((3, TILES * 128), F32),
             jax.ShapeDtypeStruct((TILES, 128), F32),
         ),
-        in_specs=[SMEM] * 4 + [VMEM] * 8,
+        in_specs=[SMEM] * 4 + [VMEM] * 3 + [ANY] * 2 + [VMEM] * 3,
         out_specs=(VMEM, VMEM),
         scratch_shapes=[
             pltpu.SMEM((TILES + 2,), jnp.int32),
             pltpu.SMEM((TILES + 2,), jnp.int32),
             pltpu.VMEM((3, (TILES + 2) * 128), F32),
             pltpu.VMEM((TILES + 2, 8, 128), F32),
+            pltpu.VMEM((CHIPS, 8, 8, 128), F32),
+            pltpu.VMEM((CHIPS, 8, 8, 128), F32),
+            pltpu.SemaphoreType.DMA((2,)),
         ],
-        compiler_params=pltpu.CompilerParams(vmem_limit_bytes=56 * 2**20),
+        compiler_params=pltpu.CompilerParams(vmem_limit_bytes=24 * 2**20),
         name="rbf_and_flux",
     )(first, count, low, high, low, high, nodes, same, other, area, nbr, old)
 
 
-def send_body(panel_ref, xyz_ref, rhs_ref, send_ref):
-    send_ref[0:128, :] = panel_ref[...]
-    send_ref[128:136, :] = jnp.zeros((8, 1024), F32)
-    send_ref[128:131, 0:128] = xyz_ref[...]
-    send_ref[131:134, 0:128] = rhs_ref[...]
+def send_body(panel_ref, xyz_ref, rhs_ref, send_ref, held_ref, sems):
+    parts = [slice(32 * i, 32 * i + 32) for i in range(4)]
+    fetches = [pltpu.make_async_copy(panel_ref.at[p], held_ref.at[p], sems.at[i]) for i, p in enumerate(parts)]
+    for fetch in fetches:
+        fetch.start()
+    held_ref[128:136, :] = jnp.zeros((8, ORDER), F32)
+    held_ref[128:131, 0:128] = xyz_ref[...]
+    held_ref[131:134, 0:128] = rhs_ref[...]
+    parts.append(slice(128, 136))
+    sends = [pltpu.make_async_copy(held_ref.at[p], send_ref.at[p], sems.at[4 + i]) for i, p in enumerate(parts)]
+    sends[4].start()
+    for fetch, send in zip(fetches, sends):
+        fetch.wait()
+        send.start()
+    for send in sends:
+        send.wait()
 
 
 def pack_send(panel, xyz, rhs):
     return pl.pallas_call(
         send_body,
         out_shape=jax.ShapeDtypeStruct((136, ORDER), F32),
-        in_specs=[VMEM] * 3,
-        out_specs=VMEM,
+        in_specs=[ANY, VMEM, VMEM],
+        out_specs=ANY,
+        scratch_shapes=[pltpu.VMEM((136, ORDER), F32), pltpu.SemaphoreType.DMA((9,))],
         name="pack_panel",
     )(panel, xyz, rhs)
 

time: 135 us -> 130 us (0.963)
  Pallas kernels: 64.5 us -> 60.6 us
    pallas_call x1, Pallas kernels: 30.9 us -> 27.4 us  [update_mesh(): pl.pallas_call(mesh_body, out_shape=(jax.ShapeDtypeStruct((3, TILES * 128...]
  transfers between devices with their start and end apart: 6 -> 6, of which waited for: 4 -> 4; matrix products, arithmetic and copies ran while one was open for 1% -> 1% of each run, Pallas kernels for 20% -> 21%
where the time goes in v3:
time: 130 us
  Pallas kernels  60.6 us (47%)
  blocking collectives  26.8 us (21%)
  starting transfers between devices  14.7 us (11%)
  between operations  14.2 us (11%)
  waiting for transfers between devices  10.9 us (8%)
  local copies, waits for them, and re-layouts  2.42 us (2%)
    pallas_call x1, Pallas kernels, update_mesh(): pl.pallas_call(mesh_body, out_shape=(jax.ShapeDtypeStruct((3, TILES * 128...  27.4 us
    all_to_all x1, blocking collectives, chips_to_all(): lax.all_to_all(copies, 'vol', 0, 0, tiled=True, axis_index_groups=groups)  26.8 us
    pallas_call x1, Pallas kernels, solve_system(): pl.pallas_call(factor_body, out_shape=(jax.ShapeDtypeStruct((ORDER, SIDE)...  17 us
    pallas_call x1, Pallas kernels, apply_products(): pl.pallas_call(products_body, out_shape=jax.ShapeDtypeStruct((128, ORDER)...  7.75 us
    all_to_all x1, starting transfers between devices, chips_to_all(): lax.all_to_all(copies, 'vol', 0, 0, tiled=True, axis_index_groups=groups)  6.53 us
    ppermute x2, starting transfers between devices, other_core(): return lax.ppermute(blocks, 'vol', [(i, i ^ 1) for i in range(2 * CHIPS)])  3.78 us
    pallas_call x1, Pallas kernels, control_weights(): pl.pallas_call(weights_body, out_shape=jax.ShapeDtypeStruct((CHIPS, 8, 8,...  3.7 us
    all_gather x1, waiting for transfers between devices, per_device(): lax.all_gather(pack_send(panel_block, ctrl_xyz, rhs_panel), 'chol', axis=...  3.54 us
  transfers between devices with their start and end apart: 6, of which 4 were waited for; matrix products, arithmetic and copies ran while one was open for 1% of the time, Pallas kernels for 21%

profile of v3, /device:TPU:1, one launch (start us, length us, event | category | flops | bytes accessed | tf_op | source)
XLA Modules:
  0.0 129.5 jit_solution(4150895452214211068)
XLA Ops:
  7.2 0.0 all-gather.3.cloned.1.call-start
  7.2 2.5 %pack_panel.1 = f32[136,1024]{1,0:T(8,128)} custom-call(f32[128,1024]{1,0:T(8,128)} %panel_ref.3, f32[3,128]{1,0:T(4,128)} %xyz_ref.1, f32[3,128]{1,0:T(4,128)} %rhs_ref.1), custom_call_target="tpu_custom_call" | custom-call | tf_op jit(solution)/shard_map/pack_panel/pallas_call | solution.py:363
  9.7 0.0 all-gather.3.cloned.1.call-update
  9.8 1.3 slice_bitcast_fusion.first_ref.tile_first_ref
  11.1 2.3 %pack_rows.1 = (f32[16,32,640]{2,1,0:T(8,128)}, f32[8,128]{1,0:T(8,128)}, f32[8,128]{1,0:T(8,128)}) custom-call(s32[64]{0:T(128)} %slice_bitcast_fusion.first_ref.tile_first_ref, s32[64]{0:T(128)} %tile_count_ref.1, f32[32,1024]{1,0:T(8,128)} %diag_ref.1, f32[3,32]{1,0:T(4,128)} %rhs_diag_ref.1, f32[3,8192]{1,0:T(4,128)} %own_ref.1), custom_call_target="tpu_custom_call" | custom-call | tf_op jit(solution)/shard_map/pack_rows/pallas_call | solution.py:402
  13.3 0.0 copy-start.9
  13.3 0.0 copy-start.8
  13.3 26.8 %all_to_all.10.same_ref = f32[16,32,640]{2,1,0:T(8,128)S(1)} all-to-all(f32[16,32,640]{2,1,0:T(8,128)} %get-tuple-element.15), channel_id=1, replica_groups={{0,2,4,6,8,10,12,14,16,18,20,22,24,26,28,30},{1,3,5,7,9,11,13,15,17,19,..., dimensions={0} | all-to-all | bytes 2621440 | tf_op jit(solution)/shard_map/all_to_all | solution.py:417
  40.2 0.0 copy-start.6
  40.2 1.8 %collective-permute-start = (f32[16,32,640]{2,1,0:T(8,128)S(1)}, f32[16,32,640]{2,1,0:T(8,128)S(1)}, u32[]{:S(2)}, u32[]{:S(2)}) collective-permute-start(f32[16,32,640]{2,1,0:T(8,128)S(1)} %all_to_all.10.same_ref), channel_id=1, source_target_pairs={{0,1},{1,0},{2,3},{3,2},{4,5},{5,4},{6,7},{7,6},{8,9},{9,8},{10,11... | collective-permute-start | bytes 3932168 | tf_op jit(solution)/shard_map/ppermute | solution.py:421
  42.0 0.0 copy-done.9
  42.0 2.1 %collective-permute-start.1 = (f32[8,128]{1,0:T(8,128)S(1)}, f32[8,128]{1,0:T(8,128)S(1)}, u32[]{:S(2)}, u32[]{:S(2)}) collective-permute-start(f32[8,128]{1,0:T(8,128)S(1)} %copy-done.9), channel_id=1, source_target_pairs={{0,1},{1,2},{2,3},{3,4},{4,5},{5,6},{6,7},{7,8},{8,9},{9,10},{10,1... | collective-permute-start | bytes 12296 | tf_op jit(solution)/shard_map/ppermute | solution.py:444
  44.1 0.0 copy-done.8
  44.1 2.2 %collective-permute-start.2 = (f32[8,128]{1,0:T(8,128)S(1)}, f32[8,128]{1,0:T(8,128)S(1)}, u32[]{:S(2)}, u32[]{:S(2)}) collective-permute-start(f32[8,128]{1,0:T(8,128)S(1)} %copy-done.8), channel_id=1, source_target_pairs={{1,0},{2,1},{3,2},{4,3},{5,4},{6,5},{7,6},{8,7},{9,8},{10,9},{11,1... | collective-permute-start | bytes 12296 | tf_op jit(solution)/shard_map/ppermute | solution.py:445
  46.3 0.0 collective-permute-done.1.low_list_ref.low_ref
  46.3 3.1 %collective-permute-done.2.high_list_ref.high_ref = f32[8,128]{1,0:T(8,128)S(1)} collective-permute-done((f32[8,128]{1,0:T(8,128)S(1)}, f32[8,128]{1,0:T(8,128)S(1)}, u32[]{:S(2)}, u32[]{:S(2)}) %collective-permute-start.2) | collective-permute-done | bytes 4128 | tf_op jit(solution)/shard_map/ppermute | solution.py:445
  49.4 0.0 collective-permute-done.other_ref
  49.4 0.0 copy-done.6
  49.4 0.0 copy-start.7
  49.4 1.1 copy-done.7
  50.5 17.0 %block_elimination.1 = (f32[1024,256]{1,0:T(8,128)}, bf16[16,1024]{1,0:T(8,128)(2,1)}) custom-call(f32[16,32,640]{2,1,0:T(8,128)} %copy-done.6, f32[16,32,640]{2,1,0:T(8,128)} %copy-done.7, f32[128,1024]{1,0:T(8,128)} %panel_ref.3), custom_call_target="tpu_custom_call" | custom-call | tf_op jit(solution)/shard_map/block_elimination/pallas_call | solution.py:136
  67.5 3.5 %all-gather.3.cloned.1.call-done = f32[1088,1024]{1,0:T(8,128)} async-done(((f32[136,1024]{1,0:T(8,128)}), f32[1088,1024]{1,0:T(8,128)}) %all-gather.3.cloned.1.call-update) | async-done | bytes 4456464 | tf_op jit(solution)/shard_map/all_gather | solution.py:440
  71.0 3.7 %control_weights.1 = f32[16,8,8,128]{3,2,1,0:T(8,128)} custom-call(bf16[16,1024]{1,0:T(8,128)(2,1)} %get-tuple-element.19.rhs_ref, f32[8,136,1024]{2,1,0:T(8,128)} %bitcast.6), custom_call_target="tpu_custom_call" | custom-call | tf_op jit(solution)/shard_map/control_weights/pallas_call | solution.py:169
  74.7 6.5 %all-to-all-start.1 = ((f32[16,8,8,128]{3,2,1,0:T(8,128)}), f32[16,8,8,128]{3,2,1,0:T(8,128)S(1)}, u32[]{:S(2)}, u32[]{:S(2)}) async-start(f32[16,8,8,128]{3,2,1,0:T(8,128)} %control_weights.1), calls=%async_computation.1 | async-start | bytes 1048576 | tf_op jit(solution)/shard_map/all_to_all | solution.py:417
  81.2 0.0 copy-start
  81.3 0.0 copy-start.1
  81.3 0.0 copy-start.2
  81.3 0.0 copy-start.3
  81.3 0.0 copy-start.4
  81.3 0.0 copy-start.5
  81.3 7.7 %trail_update.1 = f32[128,1024]{1,0:T(8,128)} custom-call(f32[1024,256]{1,0:T(8,128)} %get-tuple-element.20.x_ref, f32[8,136,1024]{2,1,0:T(8,128)} %bitcast.7, f32[128,1024]{1,0:T(8,128)} %trail_ref.1), custom_call_target="tpu_custom_call" | custom-call | flops 805306368 | bytes 6291456 | tf_op jit(solution)/shard_map/trail_update/pallas_call | solution.py:193
  89.1 2.7 %all-to-all-done.1.same_any = f32[16,8,8,128]{3,2,1,0:T(8,128)S(1)} async-done(((f32[16,8,8,128]{3,2,1,0:T(8,128)}), f32[16,8,8,128]{3,2,1,0:T(8,128)S(1)}, u32[]{:S(2)}, u32[]{:S(2)}) %all-to-all-start.1) | async-done | bytes 524320 | tf_op jit(solution)/shard_map/all_to_all | solution.py:417
  91.8 2.0 %collective-permute-start.3 = (f32[16,8,8,128]{3,2,1,0:T(8,128)S(1)}, f32[16,8,8,128]{3,2,1,0:T(8,128)S(1)}, u32[]{:S(2)}, u32[]{:S(2)}) collective-permute-start(f32[16,8,8,128]{3,2,1,0:T(8,128)S(1)} %all-to-all-done.1.same_any), channel_id=1, source_target_pairs={{0,1},{1,0},{2,3},{3,2},{4,5},{5,4},{6,7},{7,6},{8,9},{9,8},{10,11... | collective-permute-start | bytes 1572872 | tf_op jit(solution)/shard_map/ppermute | solution.py:421
  93.7 1.5 %collective-permute-done.3.other_any = f32[16,8,8,128]{3,2,1,0:T(8,128)S(1)} collective-permute-done((f32[16,8,8,128]{3,2,1,0:T(8,128)S(1)}, f32[16,8,8,128]{3,2,1,0:T(8,128)S(1)}, u32[]{:S(2)}, u32[]{:S(2)}) %collective-permute-start.3) | collective-permute-done | bytes 524320 | tf_op jit(solution)/shard_map/ppermute | solution.py:421
  95.3 0.0 copy-done
  95.3 0.0 copy-done.1
  95.3 0.0 copy-done.2
  95.3 0.0 copy-done.3
  95.3 0.0 copy-done.4
  95.3 0.0 copy-done.5
  95.3 27.4 %rbf_and_flux.1 = (f32[3,8192]{1,0:T(4,128)}, f32[64,128]{1,0:T(8,128)}) custom-call(s32[64]{0:T(128)S(1)} %copy-done.5, s32[64]{0:T(128)S(1)} %copy-done.4, f32[8,128]{1,0:T(8,128)S(1)} %collective-permute-done.1.low_list_ref.low_ref, f32[8,128]{1,0:T(8,128)S(1)} %collective-permute-done.2.high_list_ref.high_ref, ...), custom_call_target="tpu_custom_call" | custom-call | tf_op jit(solution)/shard_map/rbf_and_flux/pallas_call | solution.py:322
Async XLA Ops:
  7.2 63.8 %all-gather.3.cloned.1.call-start = ((), (), s32[]{:S(2)}) async-start(), calls=%async_computation.2 | async-start | bytes 5013504 | tf_op jit(solution)/shard_map/all_gather | solution.py:440
  13.3 28.6 %copy-start.9 = (f32[8,128]{1,0:T(8,128)S(1)}, f32[8,128]{1,0:T(8,128)}, u32[]{:S(2)}) copy-start(f32[8,128]{1,0:T(8,128)} %get-tuple-element.16) | copy-start | bytes 12292
  13.3 30.7 %copy-start.8 = (f32[8,128]{1,0:T(8,128)S(1)}, f32[8,128]{1,0:T(8,128)}, u32[]{:S(2)}) copy-start(f32[8,128]{1,0:T(8,128)} %get-tuple-element.17) | copy-start | bytes 12292
  40.2 9.2 %copy-start.6 = (f32[16,32,640]{2,1,0:T(8,128)}, f32[16,32,640]{2,1,0:T(8,128)S(1)}, u32[]{:S(2)}) copy-start(f32[16,32,640]{2,1,0:T(8,128)S(1)} %all_to_all.10.same_ref) | copy-start | bytes 3932164
  40.2 9.2 %collective-permute-start = (f32[16,32,640]{2,1,0:T(8,128)S(1)}, f32[16,32,640]{2,1,0:T(8,128)S(1)}, u32[]{:S(2)}, u32[]{:S(2)}) collective-permute-start(f32[16,32,640]{2,1,0:T(8,128)S(1)} %all_to_all.10.same_ref), channel_id=1, source_target_pairs={{0,1},{1,0},{2,3},{3,2},{4,5},{5,4},{6,7},{7,6},{8,9},{9,8},{10,11... | collective-permute-start | bytes 3932168 | tf_op jit(solution)/shard_map/ppermute | solution.py:421
  42.0 4.3 %collective-permute-start.1 = (f32[8,128]{1,0:T(8,128)S(1)}, f32[8,128]{1,0:T(8,128)S(1)}, u32[]{:S(2)}, u32[]{:S(2)}) collective-permute-start(f32[8,128]{1,0:T(8,128)S(1)} %copy-done.9), channel_id=1, source_target_pairs={{0,1},{1,2},{2,3},{3,4},{4,5},{5,6},{6,7},{7,8},{8,9},{9,10},{10,1... | collective-permute-start | bytes 12296 | tf_op jit(solution)/shard_map/ppermute | solution.py:444
  44.1 5.3 %collective-permute-start.2 = (f32[8,128]{1,0:T(8,128)S(1)}, f32[8,128]{1,0:T(8,128)S(1)}, u32[]{:S(2)}, u32[]{:S(2)}) collective-permute-start(f32[8,128]{1,0:T(8,128)S(1)} %copy-done.8), channel_id=1, source_target_pairs={{1,0},{2,1},{3,2},{4,3},{5,4},{6,5},{7,6},{8,7},{9,8},{10,9},{11,1... | collective-permute-start | bytes 12296 | tf_op jit(solution)/shard_map/ppermute | solution.py:445
  49.4 1.1 copy-start.7
  74.7 17.0 %all-to-all-start.1 = ((f32[16,8,8,128]{3,2,1,0:T(8,128)}), f32[16,8,8,128]{3,2,1,0:T(8,128)S(1)}, u32[]{:S(2)}, u32[]{:S(2)}) async-start(f32[16,8,8,128]{3,2,1,0:T(8,128)} %control_weights.1), calls=%async_computation.1 | async-start | bytes 1048576 | tf_op jit(solution)/shard_map/all_to_all | solution.py:417
  81.2 14.0 %copy-start = (f32[3,6,8192]{2,1,0:T(8,128)S(1)}, f32[3,6,8192]{2,1,0:T(8,128)}, u32[]{:S(2)}) copy-start(f32[3,6,8192]{2,1,0:T(8,128)} %area_ref.1) | copy-start | bytes 1769476
  81.3 14.0 %copy-start.1 = (f32[3,8192]{1,0:T(4,128)S(1)}, f32[3,8192]{1,0:T(4,128)}, u32[]{:S(2)}) copy-start(f32[3,8192]{1,0:T(4,128)} %own_ref.1) | copy-start | bytes 294916
  81.3 14.0 %copy-start.2 = (s32[6,8192]{1,0:T(8,128)S(1)}, s32[6,8192]{1,0:T(8,128)}, u32[]{:S(2)}) copy-start(s32[6,8192]{1,0:T(8,128)} %nbr_ref.1) | copy-start | bytes 589828
  81.3 14.0 %copy-start.3 = (f32[8192]{0:T(1024)S(1)}, f32[8192]{0:T(1024)}, u32[]{:S(2)}) copy-start(f32[8192]{0:T(1024)} %param.23) | copy-start | bytes 98308
  81.3 14.0 %copy-start.4 = (s32[64]{0:T(128)S(1)}, s32[64]{0:T(128)}, u32[]{:S(2)}) copy-start(s32[64]{0:T(128)} %tile_count_ref.1) | copy-start | bytes 772
  81.3 14.0 %copy-start.5 = (s32[64]{0:T(128)S(1)}, s32[64]{0:T(128)}, u32[]{:S(2)}) copy-start(s32[64]{0:T(128)} %slice_bitcast_fusion.first_ref.tile_first_ref) | copy-start | bytes 772
  91.8 3.5 %collective-permute-start.3 = (f32[16,8,8,128]{3,2,1,0:T(8,128)S(1)}, f32[16,8,8,128]{3,2,1,0:T(8,128)S(1)}, u32[]{:S(2)}, u32[]{:S(2)}) collective-permute-start(f32[16,8,8,128]{3,2,1,0:T(8,128)S(1)} %all-to-all-done.1.same_any), channel_id=1, source_target_pairs={{0,1},{1,0},{2,3},{3,2},{4,5},{5,4},{6,7},{7,6},{8,9},{9,8},{10,11... | collective-permute-start | bytes 1572872 | tf_op jit(solution)/shard_map/ppermute | solution.py:421
Sparse Core Ops, SparseCore 0:
  9.9 61.0 all-gather.2

commit v4 on v3

--- a/solution.py
+++ b/solution.py
@@ -154,6 +154,8 @@
 RADIUS = 1.25
 PHI_SCALE = 4.0 * 0.8**5
 UNROLL = 11
+COMMON = 5
+MARGIN = 1e-3
 
 
 def weights_body(rhs_ref, rows_ref, ctrl_ref):
@@ -207,37 +209,132 @@
     )(x, rows, trail)
 
 
-def tile_sum(t, first_ref, count_ref, nodes_ref, same_ref, other_ref):
-    here = pl.ds(pl.multiple_of(t * 128, 128), 128)
-    core = lax.axis_index("vol") % 2
-    first = first_ref[t]
-    count = count_ref[t]
-    spread = [
-        jnp.broadcast_to(nodes_ref[a : a + 1, here], (128, 128)).T for a in range(3)
-    ]
-    highs, lows, weights = [], [], []
+def order_body(nodes_ref, low_ref, high_ref, sorted_ref, rank_ref, start_ref, stop_ref):
+    down = lax.broadcasted_iota(jnp.int32, (128, 128), 0)
+    along = lax.broadcasted_iota(jnp.int32, (128, 128), 1)
+
+    def order_tile(t, xyz):
+        row = jnp.broadcast_to(xyz[0:1], (128, 128))
+        column = row.T
+        before = (column < row) | ((column == row) & (down < along))
+        rank = jnp.sum(before.astype(F32), axis=0, keepdims=True)
+        rank_column = jnp.broadcast_to(rank, (128, 128)).T
+        order = jnp.sum(jnp.where(rank_column == along.astype(F32), down.astype(F32), 0.0), axis=0, keepdims=True)
+        order = jnp.broadcast_to(order.astype(jnp.int32), (8, 128))
+        full = jnp.concatenate([xyz, jnp.zeros((5, 128), F32)], axis=0)
+        full = jnp.take_along_axis(full, order, axis=1, mode="promise_in_bounds")
+        sorted_ref[t] = full
+        rank_ref[t] = jnp.broadcast_to(rank.astype(jnp.int32), (8, 128))
+        start_ref[pl.ds(t, 1), :] = jnp.floor(full[0:1] - (RADIUS + MARGIN)).astype(jnp.int32)
+        stop_ref[pl.ds(t, 1), :] = jnp.floor(full[0:1] + (RADIUS + MARGIN)).astype(jnp.int32)
+
+    order_tile(0, low_ref[0:3])
+    order_tile(TILES + 1, high_ref[0:3])
+
+    def several(i, carry):
+        for u in range(16):
+            t = 16 * i + u
+            order_tile(t + 1, nodes_ref[:, pl.ds(pl.multiple_of(t * 128, 128), 128)])
+        return carry
+
+    lax.fori_loop(0, TILES // 16, several, 0)
+
+
+def order_nodes(nodes, low, high):
+    ids = jax.ShapeDtypeStruct((TILES + 2, 128), jnp.int32)
+    return pl.pallas_call(
+        order_body,
+        out_shape=(
+            jax.ShapeDtypeStruct((TILES + 2, 8, 128), F32),
+            jax.ShapeDtypeStruct((TILES + 2, 8, 128), jnp.int32),
+            ids,
+            ids,
+        ),
+        in_specs=[VMEM] * 3,
+        out_specs=(VMEM,) * 4,
+        cost_estimate=pl.CostEstimate(flops=20_000_000, bytes_accessed=2**20, transcendentals=0),
+        name="node_order",
+    )(nodes, low, high)
+
+
+def phi_of(dist_sq):
+    dist = dist_sq * lax.rsqrt(jnp.maximum(dist_sq, 1e-30))
+    remain = jnp.maximum(RADIUS - dist, 0.0)
+    remain_sq = remain * remain
+    return remain_sq * remain_sq * (RADIUS * RADIUS - remain)
+
+
+def group_phi(spread, ctrl_ref, blocks):
+    dist_sq = None
+    for a in range(3):
+        differ = jnp.concatenate(
+            [spread[a][16 * g : 16 * g + 16] - ctrl_ref[blocks[g], a : a + 1, :] for g in range(8)], axis=0
+        )
+        dist_sq = differ * differ if a == 0 else dist_sq + differ * differ
+    return split(phi_of(dist_sq))
+
+
+def group_sums(weight, high, low, rank):
+    weight = weight.astype(BF16)
+    both = raw_dot(weight, low, NT) + raw_dot(weight, high, NT)
+    group_of = lax.broadcasted_iota(jnp.int32, (8, 128), 1) // 16
+    total = jnp.zeros((8, 128), F32)
+    for g in range(8):
+        total = jnp.where(group_of == g, both[8 * g : 8 * g + 8], total)
+    total = (total + pltpu.roll(total, 3, axis=0)) * PHI_SCALE
+    return jnp.take_along_axis(total, rank, axis=1, mode="promise_in_bounds")
+
+
+def node_columns(sorted_ref, t):
+    return [jnp.broadcast_to(sorted_ref[t, a : a + 1, :], (128, 128)).T for a in range(3)]
+
+
+def group_starts(t, first, start_ref):
+    return [jnp.clip(start_ref[t, 16 * g] - first, 0, SLOTS - 1) for g in range(8)]
+
+
+def tile_sum(t, u, first, count, start_ref, stop_ref, sorted_ref, rank_ref, ctrl_ref, weight_ref):
+    row_id = lax.broadcasted_iota(jnp.int32, (8, 128), 0)
     for s in range(SLOTS):
         live = s < count
-        block = jnp.where(live, first + s, first)
-        chip, rank = (block // 2) % CHIPS, block // 32
-        ctrl = jnp.where(block % 2 == core, same_ref[chip, rank], other_ref[chip, rank])
-        dist_sq = jnp.zeros((128, 128), F32)
-        for a in range(3):
-            differ = spread[a] - ctrl[a : a + 1, :]
-            dist_sq = dist_sq + differ * differ
-        dist = dist_sq * lax.rsqrt(jnp.maximum(dist_sq, 1e-30))
-        remain = jnp.maximum(RADIUS - dist, 0.0)
-        remain_sq = remain * remain
-        phi = remain_sq * remain_sq * (RADIUS * RADIUS - remain)
-        high, low = split(phi)
-        highs.append(high)
-        lows.append(low)
-        w_high, w_low = split(jnp.where(live, ctrl, 0.0))
-        weights.append(jnp.concatenate([w_high, w_low], axis=0))
-    weight = jnp.concatenate(weights, axis=1)
-    by_high = raw_dot(weight, jnp.concatenate(highs, axis=1), NT)
-    by_low = raw_dot(weight, jnp.concatenate(lows, axis=1), NT)
-    return (by_low[0:8] + by_high[8:16] + by_high[0:8]) * PHI_SCALE
+        ctrl = ctrl_ref[jnp.where(live, first + s, first)]
+        ctrl = jnp.where(live, ctrl, 0.0)
+        high = ctrl.astype(BF16).astype(F32)
+        low = pltpu.roll(ctrl - high, 5, axis=0)
+        weight_ref[u, :, 128 * s : 128 * s + 128] = jnp.where(row_id < 3, low, jnp.where(row_id < 6, high, 0.0))
+    starts = group_starts(t, first, start_ref)
+    most = jnp.int32(0)
+    for g in range(8):
+        most = jnp.maximum(most, jnp.clip(stop_ref[t, 16 * g + 15] - first, 0, count - 1) - starts[g] + 1)
+    spread = node_columns(sorted_ref, t)
+    parts = [
+        group_phi(spread, ctrl_ref, [jnp.minimum(first + starts[g] + j, 255) for g in range(8)]) for j in range(COMMON)
+    ]
+    weight = jnp.concatenate(
+        [weight_ref[u, :, pl.ds(pl.multiple_of(starts[g] * 128, 128), COMMON * 128)] for g in range(8)], axis=0
+    )
+    high = jnp.concatenate([part[0] for part in parts], axis=1)
+    low = jnp.concatenate([part[1] for part in parts], axis=1)
+    return group_sums(weight, high, low, rank_ref[t]), most
+
+
+def tile_rest(t, u, first, most, start_ref, sorted_ref, rank_ref, ctrl_ref, weight_ref, d_ref):
+    starts = group_starts(t, first, start_ref)
+
+    def step(j, carry):
+        spread = node_columns(sorted_ref, t)
+        high, low = group_phi(spread, ctrl_ref, [jnp.minimum(first + starts[g] + j, 255) for g in range(8)])
+        weight = jnp.concatenate(
+            [
+                weight_ref[u, :, pl.ds(pl.multiple_of(jnp.minimum(starts[g] + j, SLOTS) * 128, 128), 128)]
+                for g in range(8)
+            ],
+            axis=0,
+        )
+        d_ref[t] = d_ref[t] + group_sums(weight, high, low, rank_ref[t])
+        return carry
+
+    lax.fori_loop(COMMON, most, step, 0)
 
 
 def mesh_body(
@@ -245,9 +342,10 @@
     tile_count_ref,
     low_list_ref,
     high_list_ref,
-    low_ref,
-    high_ref,
-    own_ref,
+    start_ref,
+    stop_ref,
+    sorted_ref,
+    rank_ref,
     same_any,
     other_any,
     area_ref,
@@ -257,10 +355,12 @@
     volume_ref,
     first_ref,
     count_ref,
-    nodes_ref,
+    most_ref,
     d_ref,
     same_ref,
     other_ref,
+    ctrl_ref,
+    weight_ref,
     sems,
 ):
     copies = [
@@ -271,7 +371,7 @@
         copy.start()
 
     def lists(t, carry):
-        first_ref[t + 1] = tile_first_ref[t]
+        first_ref[t + 1] = tile_first_ref[0, t]
         count_ref[t + 1] = tile_count_ref[t]
         return carry
 
@@ -279,9 +379,7 @@
     for t, list_ref in ((0, low_list_ref), (TILES + 1, high_list_ref)):
         first_ref[t] = list_ref[3, 0].astype(jnp.int32)
         count_ref[t] = list_ref[3, 1].astype(jnp.int32)
-    nodes_ref[:, 0:128] = low_ref[0:3]
-    nodes_ref[:, 128 : 128 + TILES * 128] = own_ref[...]
-    nodes_ref[:, 128 + TILES * 128 :] = high_ref[0:3]
+    weight_ref[:, :, SLOTS * 128 :] = jnp.zeros((UNROLL, 8, COMMON * 128), F32)
 
     def flux_tile(t):
         here = pl.ds(pl.multiple_of(t * 128, 128), 128)
@@ -305,40 +403,64 @@
     def sums(i, carry):
         for u in range(UNROLL):
             flux_tile(jnp.maximum((i - 1) * UNROLL + u - 2, 0))
+        most = jnp.int32(0)
         for u in range(UNROLL):
             t = i * UNROLL + u
-            d_ref[t] = tile_sum(t, first_ref, count_ref, nodes_ref, same_ref, other_ref)
+            d_ref[t], need = tile_sum(
+                t, u, first_ref[t], count_ref[t], start_ref, stop_ref, sorted_ref, rank_ref, ctrl_ref, weight_ref
+            )
+            most_ref[u] = need
+            most = jnp.maximum(most, need)
+
+        @pl.when(most > COMMON)
+        def _():
+            def rest(u, carry):
+                t = i * UNROLL + u
+                tile_rest(
+                    t, u, first_ref[t], most_ref[u], start_ref, sorted_ref, rank_ref, ctrl_ref, weight_ref, d_ref
+                )
+                return carry
+
+            lax.fori_loop(0, UNROLL, rest, 0)
+
         return carry
 
     d_ref[0:3] = jnp.zeros((3, 8, 128), F32)
     for copy in copies:
         copy.wait()
+    core = lax.axis_index("vol") % 2
+    for chip in range(CHIPS):
+        for rank in range(8):
+            ctrl_ref[32 * rank + 2 * chip + core] = same_ref[chip, rank]
+            ctrl_ref[32 * rank + 2 * chip + 1 - core] = other_ref[chip, rank]
     lax.fori_loop(0, (TILES + 2) // UNROLL, sums, 0)
     for u in range(UNROLL):
         flux_tile(TILES - UNROLL + u)
 
 
-def update_mesh(first, count, low, high, nodes, same, other, area, nbr, old):
+def update_mesh(first, count, low, high, start, stop, nodes, rank, same, other, area, nbr, old):
     return pl.pallas_call(
         mesh_body,
         out_shape=(
             jax.ShapeDtypeStruct((3, TILES * 128), F32),
             jax.ShapeDtypeStruct((TILES, 128), F32),
         ),
-        in_specs=[SMEM] * 4 + [VMEM] * 3 + [ANY] * 2 + [VMEM] * 3,
+        in_specs=[SMEM] * 6 + [VMEM] * 2 + [ANY] * 2 + [VMEM] * 3,
         out_specs=(VMEM, VMEM),
         scratch_shapes=[
             pltpu.SMEM((TILES + 2,), jnp.int32),
             pltpu.SMEM((TILES + 2,), jnp.int32),
-            pltpu.VMEM((3, (TILES + 2) * 128), F32),
+            pltpu.SMEM((UNROLL,), jnp.int32),
             pltpu.VMEM((TILES + 2, 8, 128), F32),
             pltpu.VMEM((CHIPS, 8, 8, 128), F32),
             pltpu.VMEM((CHIPS, 8, 8, 128), F32),
+            pltpu.VMEM((256, 8, 128), F32),
+            pltpu.VMEM((UNROLL, 8, (SLOTS + COMMON) * 128), F32),
             pltpu.SemaphoreType.DMA((2,)),
         ],
-        compiler_params=pltpu.CompilerParams(vmem_limit_bytes=24 * 2**20),
+        compiler_params=pltpu.CompilerParams(vmem_limit_bytes=32 * 2**20),
         name="rbf_and_flux",
-    )(first, count, low, high, low, high, nodes, same, other, area, nbr, old)
+    )(first, count, low, high, start, stop, nodes, rank, same, other, area, nbr, old)
 
 
 def send_body(panel_ref, xyz_ref, rhs_ref, send_ref, held_ref, sems):
@@ -390,7 +512,7 @@
     row_id = lax.broadcasted_iota(jnp.int32, (8, 128), 0)
     lane = lax.broadcasted_iota(jnp.int32, (8, 128), 1)
     for edge_ref, tile in ((head_ref, 0), (tail_ref, TILES - 1)):
-        first = first_ref[tile].astype(F32)
+        first = first_ref[0, tile].astype(F32)
         count = count_ref[tile].astype(F32)
         lists = jnp.where(lane == 0, first, jnp.where(lane == 1, count, 0.0))
         edge_ref[...] = jnp.where(row_id == 3, lists, 0.0)
@@ -435,7 +557,7 @@
     edge_nbr,
     old_volume,
 ):
-    firsts = tile_blocks[:, 0]
+    firsts = tile_blocks.T
     rows, head, tail = pack(firsts, tile_count, diag_block, rhs_diag, node_xyz)
     column_rows = lax.all_gather(pack_send(panel_block, ctrl_xyz, rhs_panel), "chol", axis=0, tiled=False)
     same_rows = chips_to_all(rows)
@@ -444,13 +566,15 @@
     low = lax.ppermute(tail, "vol", [(i, i + 1) for i in range(size - 1)])
     high = lax.ppermute(head, "vol", [(i + 1, i) for i in range(size - 1)])
     other_rows, low, high = lax.optimization_barrier((other_rows, low, high))
+    in_order, ranks, start, stop = order_nodes(node_xyz, low, high)
     x, rhs_solved = solve_system(same_rows, other_rows, panel_block)
+    rhs_solved, in_order, ranks, start, stop = lax.optimization_barrier((rhs_solved, in_order, ranks, start, stop))
     same_ctrl = chips_to_all(control_weights(rhs_solved, column_rows))
     trail_out = apply_products(x, column_rows, trail)
     same_ctrl, trail_out = lax.optimization_barrier((same_ctrl, trail_out))
     other_ctrl = other_core(same_ctrl)
     node_disp, new_volume = update_mesh(
-        firsts, tile_count, low, high, node_xyz, same_ctrl, other_ctrl, face_area, edge_nbr, old_volume.reshape(TILES, 128)
+        firsts, tile_count, low, high, start, stop, in_order, ranks, same_ctrl, other_ctrl, face_area, edge_nbr, old_volume.reshape(TILES, 128)
     )
     return (trail_out, node_disp, new_volume.reshape(-1))
 

time: 130 us -> 130 us (level)
  the two profiles are of different devices: /device:TPU:1 before, /device:TPU:0 now
where the time goes in v4:
time: 130 us
  Pallas kernels  68.7 us (53%)
  blocking collectives  25.4 us (20%)
  between operations  14.3 us (11%)
  starting transfers between devices  10.7 us (8%)
  waiting for transfers between devices  9.39 us (7%)
    pallas_call x1, Pallas kernels, update_mesh(): pl.pallas_call(mesh_body, out_shape=(jax.ShapeDtypeStruct((3, TILES * 128...  29.1 us
    all_to_all x1, blocking collectives, chips_to_all(): lax.all_to_all(copies, 'vol', 0, 0, tiled=True, axis_index_groups=groups)  25.4 us
    pallas_call x1, Pallas kernels, solve_system(): pl.pallas_call(factor_body, out_shape=(jax.ShapeDtypeStruct((ORDER, SIDE)...  17 us
    pallas_call x1, Pallas kernels, apply_products(): pl.pallas_call(products_body, out_shape=jax.ShapeDtypeStruct((128, ORDER)...  7.76 us
    all_to_all x1, starting transfers between devices, chips_to_all(): lax.all_to_all(copies, 'vol', 0, 0, tiled=True, axis_index_groups=groups)  6.81 us
    pallas_call x1, Pallas kernels, order_nodes(): pl.pallas_call(order_body, out_shape=(jax.ShapeDtypeStruct((TILES + 2, 8,...  6.34 us
    all_to_all x1, waiting for transfers between devices, chips_to_all(): lax.all_to_all(copies, 'vol', 0, 0, tiled=True, axis_index_groups=groups)  4.75 us
    pallas_call x1, Pallas kernels, control_weights(): pl.pallas_call(weights_body, out_shape=jax.ShapeDtypeStruct((CHIPS, 8, 8,...  3.72 us
  transfers between devices with their start and end apart: 6, of which 4 were waited for; matrix products, arithmetic and copies ran while one was open for 0% of the time, Pallas kernels for 26%

profile of v4, /device:TPU:0, one launch (start us, length us, event | category | flops | bytes accessed | tf_op | source)
XLA Modules:
  0.0 129.6 jit_solution(16618241411891548860)
XLA Ops:
  7.2 0.0 all-gather.3.cloned.1.call-start
  7.2 2.5 %pack_panel.1 = f32[136,1024]{1,0:T(8,128)} custom-call(f32[128,1024]{1,0:T(8,128)} %panel_ref.3, f32[3,128]{1,0:T(4,128)} %xyz_ref.1, f32[3,128]{1,0:T(4,128)} %rhs_ref.1), custom_call_target="tpu_custom_call" | custom-call | tf_op jit(solution)/shard_map/pack_panel/pallas_call | solution.py:485
  9.8 0.0 all-gather.3.cloned.1.call-update
  9.8 2.3 %pack_rows.1 = (f32[16,32,640]{2,1,0:T(8,128)}, f32[8,128]{1,0:T(8,128)}, f32[8,128]{1,0:T(8,128)}) custom-call(s32[8,64]{1,0:T(8,128)} %bitcast.5, s32[64]{0:T(128)} %tile_count_ref.1, f32[32,1024]{1,0:T(8,128)} %diag_ref.1, f32[3,32]{1,0:T(4,128)} %rhs_diag_ref.1, f32[3,8192]{1,0:T(4,128)} %nodes_ref.3), custom_call_target="tpu_custom_call" | custom-call | tf_op jit(solution)/shard_map/pack_rows/pallas_call | solution.py:524
  12.0 0.0 copy-start.16
  12.0 0.0 copy-start.15
  12.0 25.4 %all_to_all.10.same_ref = f32[16,32,640]{2,1,0:T(8,128)S(1)} all-to-all(f32[16,32,640]{2,1,0:T(8,128)} %get-tuple-element.24), channel_id=1, replica_groups={{0,2,4,6,8,10,12,14,16,18,20,22,24,26,28,30},{1,3,5,7,9,11,13,15,17,19,..., dimensions={0} | all-to-all | bytes 2621440 | tf_op jit(solution)/shard_map/all_to_all | solution.py:539
  37.4 0.0 copy-start.13
  37.4 0.0 collective-permute-start
  37.4 0.0 copy-done.16
  37.5 2.4 %collective-permute-start.1 = (f32[8,128]{1,0:T(8,128)S(1)}, f32[8,128]{1,0:T(8,128)S(1)}, u32[]{:S(2)}, u32[]{:S(2)}) collective-permute-start(f32[8,128]{1,0:T(8,128)S(1)} %copy-done.16), channel_id=1, source_target_pairs={{0,1},{1,2},{2,3},{3,4},{4,5},{5,6},{6,7},{7,8},{8,9},{9,10},{10,1... | collective-permute-start | bytes 12296 | tf_op jit(solution)/shard_map/ppermute | solution.py:566
  39.9 0.0 copy-done.15
  39.9 1.3 collective-permute-start.2
  41.2 0.0 collective-permute-done.1.low_ref.low_list_ref
  41.2 0.0 copy-start.8
  41.2 1.7 %collective-permute-done.2.high_ref.high_list_ref = f32[8,128]{1,0:T(8,128)S(1)} collective-permute-done((f32[8,128]{1,0:T(8,128)S(1)}, f32[8,128]{1,0:T(8,128)S(1)}, u32[]{:S(2)}, u32[]{:S(2)}) %collective-permute-start.2) | collective-permute-done | bytes 4128 | tf_op jit(solution)/shard_map/ppermute | solution.py:567
  42.9 0.0 copy-start.10
  42.9 0.0 collective-permute-done.other_ref
  42.9 0.0 copy-done.13
  42.9 0.0 copy-start.14
  43.0 1.1 copy-done.14
  44.0 17.0 %block_elimination.1 = (f32[1024,256]{1,0:T(8,128)}, bf16[16,1024]{1,0:T(8,128)(2,1)}) custom-call(f32[16,32,640]{2,1,0:T(8,128)} %copy-done.13, f32[16,32,640]{2,1,0:T(8,128)} %copy-done.14, f32[128,1024]{1,0:T(8,128)} %panel_ref.3), custom_call_target="tpu_custom_call" | custom-call | tf_op jit(solution)/shard_map/block_elimination/pallas_call | solution.py:136
  61.0 0.0 copy-done.8
  61.0 0.0 copy-done.10
  61.0 6.3 %node_order.1 = (f32[66,8,128]{2,1,0:T(8,128)}, s32[66,8,128]{2,1,0:T(8,128)}, s32[66,128]{1,0:T(8,128)}, s32[66,128]{1,0:T(8,128)}) custom-call(f32[3,8192]{1,0:T(4,128)} %nodes_ref.3, f32[8,128]{1,0:T(8,128)} %copy-done.8, f32[8,128]{1,0:T(8,128)} %copy-done.10), custom_call_target="tpu_custom_call" | custom-call | flops 20000000 | bytes 1048576 | tf_op jit(solution)/shard_map/node_order/pallas_call | solution.py:245
  67.3 1.1 all-gather.3.cloned.1.call-done
  68.5 3.7 %control_weights.1 = f32[16,8,8,128]{3,2,1,0:T(8,128)} custom-call(bf16[16,1024]{1,0:T(8,128)(2,1)} %get-tuple-element.35.rhs_ref, f32[8,136,1024]{2,1,0:T(8,128)} %bitcast.7), custom_call_target="tpu_custom_call" | custom-call | tf_op jit(solution)/shard_map/control_weights/pallas_call | solution.py:171
  72.2 6.8 %all-to-all-start.1 = ((f32[16,8,8,128]{3,2,1,0:T(8,128)}), f32[16,8,8,128]{3,2,1,0:T(8,128)S(1)}, u32[]{:S(2)}, u32[]{:S(2)}) async-start(f32[16,8,8,128]{3,2,1,0:T(8,128)} %control_weights.1), calls=%async_computation.1 | async-start | bytes 1048576 | tf_op jit(solution)/shard_map/all_to_all | solution.py:539
  79.0 0.0 copy-start
  79.0 0.0 copy-start.1
  79.0 0.0 copy-start.2
  79.0 0.0 copy-start.3
  79.0 0.0 copy-start.4
  79.0 0.0 copy-start.5
  79.1 0.0 copy-start.6
  79.1 0.0 copy-start.7
  79.1 0.0 copy-start.9
  79.1 0.0 copy-start.11
  79.1 0.0 copy-start.12
  79.1 7.8 %trail_update.1 = f32[128,1024]{1,0:T(8,128)} custom-call(f32[1024,256]{1,0:T(8,128)} %get-tuple-element.36.x_ref, f32[8,136,1024]{2,1,0:T(8,128)} %bitcast.8, f32[128,1024]{1,0:T(8,128)} %trail_ref.1), custom_call_target="tpu_custom_call" | custom-call | flops 805306368 | bytes 6291456 | tf_op jit(solution)/shard_map/trail_update/pallas_call | solution.py:195
  86.9 4.7 %all-to-all-done.1.same_any = f32[16,8,8,128]{3,2,1,0:T(8,128)S(1)} async-done(((f32[16,8,8,128]{3,2,1,0:T(8,128)}), f32[16,8,8,128]{3,2,1,0:T(8,128)S(1)}, u32[]{:S(2)}, u32[]{:S(2)}) %all-to-all-start.1) | async-done | bytes 524320 | tf_op jit(solution)/shard_map/all_to_all | solution.py:539
  91.6 0.1 collective-permute-start.3
  91.8 1.8 %collective-permute-done.3.other_any = f32[16,8,8,128]{3,2,1,0:T(8,128)S(1)} collective-permute-done((f32[16,8,8,128]{3,2,1,0:T(8,128)S(1)}, f32[16,8,8,128]{3,2,1,0:T(8,128)S(1)}, u32[]{:S(2)}, u32[]{:S(2)}) %collective-permute-start.3) | collective-permute-done | bytes 524320 | tf_op jit(solution)/shard_map/ppermute | solution.py:543
  93.5 0.0 copy-done
  93.5 0.0 copy-done.1
  93.5 0.0 copy-done.2
  93.5 0.0 copy-done.3
  93.5 0.0 copy-done.4
  93.6 0.0 copy-done.5
  93.6 0.0 copy-done.6
  93.6 0.0 copy-done.7
  93.6 0.0 copy-done.9
  93.6 0.0 copy-done.11
  93.6 0.0 copy-done.12
  93.6 29.1 %rbf_and_flux.1 = (f32[3,8192]{1,0:T(4,128)}, f32[64,128]{1,0:T(8,128)}) custom-call(s32[8,64]{1,0:T(8,128)S(1)} %bitcast.6, s32[64]{0:T(128)S(1)} %copy-done.12, f32[8,128]{1,0:T(8,128)S(1)} %copy-done.9, f32[8,128]{1,0:T(8,128)S(1)} %copy-done.11, s32[66,128]{1,0:T(8,128)S(1)} %copy-done.4, s32[66,128]{1,0:T(8,128)S(1)} %copy-done.5, ...), custom_call_target="tpu_custom_call" | custom-call | tf_op jit(solution)/shard_map/rbf_and_flux/pallas_call | solution.py:442
Async XLA Ops:
  7.2 61.3 %all-gather.3.cloned.1.call-start = ((), (), s32[]{:S(2)}) async-start(), calls=%async_computation.2 | async-start | bytes 5013504 | tf_op jit(solution)/shard_map/all_gather | solution.py:562
  12.0 25.4 %copy-start.16 = (f32[8,128]{1,0:T(8,128)S(1)}, f32[8,128]{1,0:T(8,128)}, u32[]{:S(2)}) copy-start(f32[8,128]{1,0:T(8,128)} %get-tuple-element.25) | copy-start | bytes 12292
  12.0 27.8 %copy-start.15 = (f32[8,128]{1,0:T(8,128)S(1)}, f32[8,128]{1,0:T(8,128)}, u32[]{:S(2)}) copy-start(f32[8,128]{1,0:T(8,128)} %get-tuple-element.26) | copy-start | bytes 12292
  37.4 5.5 %copy-start.13 = (f32[16,32,640]{2,1,0:T(8,128)}, f32[16,32,640]{2,1,0:T(8,128)S(1)}, u32[]{:S(2)}) copy-start(f32[16,32,640]{2,1,0:T(8,128)S(1)} %all_to_all.10.same_ref) | copy-start | bytes 3932164
  37.4 5.5 %collective-permute-start = (f32[16,32,640]{2,1,0:T(8,128)S(1)}, f32[16,32,640]{2,1,0:T(8,128)S(1)}, u32[]{:S(2)}, u32[]{:S(2)}) collective-permute-start(f32[16,32,640]{2,1,0:T(8,128)S(1)} %all_to_all.10.same_ref), channel_id=1, source_target_pairs={{0,1},{1,0},{2,3},{3,2},{4,5},{5,4},{6,7},{7,6},{8,9},{9,8},{10,11... | collective-permute-start | bytes 3932168 | tf_op jit(solution)/shard_map/ppermute | solution.py:543
  37.5 3.7 %collective-permute-start.1 = (f32[8,128]{1,0:T(8,128)S(1)}, f32[8,128]{1,0:T(8,128)S(1)}, u32[]{:S(2)}, u32[]{:S(2)}) collective-permute-start(f32[8,128]{1,0:T(8,128)S(1)} %copy-done.16), channel_id=1, source_target_pairs={{0,1},{1,2},{2,3},{3,4},{4,5},{5,6},{6,7},{7,8},{8,9},{9,10},{10,1... | collective-permute-start | bytes 12296 | tf_op jit(solution)/shard_map/ppermute | solution.py:566
  39.9 3.1 %collective-permute-start.2 = (f32[8,128]{1,0:T(8,128)S(1)}, f32[8,128]{1,0:T(8,128)S(1)}, u32[]{:S(2)}, u32[]{:S(2)}) collective-permute-start(f32[8,128]{1,0:T(8,128)S(1)} %copy-done.15), channel_id=1, source_target_pairs={{1,0},{2,1},{3,2},{4,3},{5,4},{6,5},{7,6},{8,7},{9,8},{10,9},{11,1... | collective-permute-start | bytes 12296 | tf_op jit(solution)/shard_map/ppermute | solution.py:567
  41.2 19.8 %copy-start.8 = (f32[8,128]{1,0:T(8,128)}, f32[8,128]{1,0:T(8,128)S(1)}, u32[]{:S(2)}) copy-start(f32[8,128]{1,0:T(8,128)S(1)} %collective-permute-done.1.low_ref.low_list_ref) | copy-start | bytes 12292
  42.9 18.1 %copy-start.10 = (f32[8,128]{1,0:T(8,128)}, f32[8,128]{1,0:T(8,128)S(1)}, u32[]{:S(2)}) copy-start(f32[8,128]{1,0:T(8,128)S(1)} %collective-permute-done.2.high_ref.high_list_ref) | copy-start | bytes 12292
  42.9 1.1 copy-start.14
  72.2 19.4 %all-to-all-start.1 = ((f32[16,8,8,128]{3,2,1,0:T(8,128)}), f32[16,8,8,128]{3,2,1,0:T(8,128)S(1)}, u32[]{:S(2)}, u32[]{:S(2)}) async-start(f32[16,8,8,128]{3,2,1,0:T(8,128)} %control_weights.1), calls=%async_computation.1 | async-start | bytes 1048576 | tf_op jit(solution)/shard_map/all_to_all | solution.py:539
  79.0 14.5 %copy-start = (f32[3,6,8192]{2,1,0:T(8,128)S(1)}, f32[3,6,8192]{2,1,0:T(8,128)}, u32[]{:S(2)}) copy-start(f32[3,6,8192]{2,1,0:T(8,128)} %area_ref.1) | copy-start | bytes 1769476
  79.0 14.5 %copy-start.1 = (f32[66,8,128]{2,1,0:T(8,128)S(1)}, f32[66,8,128]{2,1,0:T(8,128)}, u32[]{:S(2)}) copy-start(f32[66,8,128]{2,1,0:T(8,128)} %get-tuple-element.40.sorted_ref) | copy-start | bytes 811012
  79.0 14.5 %copy-start.2 = (s32[66,8,128]{2,1,0:T(8,128)S(1)}, s32[66,8,128]{2,1,0:T(8,128)}, u32[]{:S(2)}) copy-start(s32[66,8,128]{2,1,0:T(8,128)} %get-tuple-element.41.rank_ref) | copy-start | bytes 811012
  79.0 14.5 %copy-start.3 = (s32[6,8192]{1,0:T(8,128)S(1)}, s32[6,8192]{1,0:T(8,128)}, u32[]{:S(2)}) copy-start(s32[6,8192]{1,0:T(8,128)} %nbr_ref.1) | copy-start | bytes 589828
  79.0 14.5 %copy-start.4 = (s32[66,128]{1,0:T(8,128)S(1)}, s32[66,128]{1,0:T(8,128)}, u32[]{:S(2)}) copy-start(s32[66,128]{1,0:T(8,128)} %get-tuple-element.38.start_ref) | copy-start | bytes 101380
  79.0 14.5 %copy-start.5 = (s32[66,128]{1,0:T(8,128)S(1)}, s32[66,128]{1,0:T(8,128)}, u32[]{:S(2)}) copy-start(s32[66,128]{1,0:T(8,128)} %get-tuple-element.39.stop_ref) | copy-start | bytes 101380
  79.1 14.5 %copy-start.6 = (f32[8192]{0:T(1024)S(1)}, f32[8192]{0:T(1024)}, u32[]{:S(2)}) copy-start(f32[8192]{0:T(1024)} %param.23) | copy-start | bytes 98308
  79.1 14.5 %copy-start.7 = (s32[64,8]{0,1:T(8,128)S(1)}, s32[64,8]{0,1:T(8,128)}, u32[]{:S(2)}) copy-start(s32[64,8]{0,1:T(8,128)} %param.19) | copy-start | bytes 6148
  79.1 14.5 %copy-start.9 = (f32[8,128]{1,0:T(8,128)S(1)}, f32[8,128]{1,0:T(8,128)}, u32[]{:S(2)}) copy-start(f32[8,128]{1,0:T(8,128)} %copy-done.8) | copy-start | bytes 12292
  79.1 14.5 %copy-start.11 = (f32[8,128]{1,0:T(8,128)S(1)}, f32[8,128]{1,0:T(8,128)}, u32[]{:S(2)}) copy-start(f32[8,128]{1,0:T(8,128)} %copy-done.10) | copy-start | bytes 12292
  79.1 14.5 %copy-start.12 = (s32[64]{0:T(128)S(1)}, s32[64]{0:T(128)}, u32[]{:S(2)}) copy-start(s32[64]{0:T(128)} %tile_count_ref.1) | copy-start | bytes 772
  91.6 1.9 %collective-permute-start.3 = (f32[16,8,8,128]{3,2,1,0:T(8,128)S(1)}, f32[16,8,8,128]{3,2,1,0:T(8,128)S(1)}, u32[]{:S(2)}, u32[]{:S(2)}) collective-permute-start(f32[16,8,8,128]{3,2,1,0:T(8,128)S(1)} %all-to-all-done.1.same_any), channel_id=1, source_target_pairs={{0,1},{1,0},{2,3},{3,2},{4,5},{5,4},{6,7},{7,6},{8,9},{9,8},{10,11... | collective-permute-start | bytes 1572872 | tf_op jit(solution)/shard_map/ppermute | solution.py:543
Sparse Core Ops, SparseCore 0:
  9.9 58.4 all-gather.2
